TPU v7x, 512 devices: a whole 4x4x16 slice. The times are simulated.
512 devices in a mesh: chan: 64 (over z, y), rad: 8 (over x, core).
Axes of the slice: x: 4, y: 4, z: 16, core: 2. Of those that a mesh axis runs over, the one named last changes fastest.
Arguments:
- trial_block: float32 [1024, 16, 128], P('chan', None, 'rad')
- ham_blocks: bfloat16 [1024, 8, 128, 128], P('chan', None, 'rad'), may hold values from -0.1875 to 0.1875
- partners: int32 [1024, 8], P('chan'), may hold values from 0 to 1023, as said below
- stored_at: int32 [1024], replicated, may hold values from 0 to 1023, as said below
- precond_diag: float32 [1024, 128], P('chan', 'rad'), may hold values from 1 to 10
Outputs:
- new_block: float32 [1024, 16, 128], P('chan', None, 'rad')
- ritz_values: float32 [16], replicated
Inputs may be any that keep to these rules, and one draw needn't show every extreme that they name: `stored_at`: A permutation of the channel numbers. `partners`: among the 128 entries of the rows p with p // 16 = d, for every d, at most 4 have stored_at[partner] // 16 equal to any one value; for every d some value has exactly 4.
All inputs are finite; a program needn't handle non-finite values.
Results may differ from a plain program's by a relative error of at most 0.0051.
Values may be sent and summed in bfloat16 or wider, within the bound.
A program may use at most 64 MiB of HBM per device.

v0:
```python
import jax
import jax.numpy as jnp
from jax import lax
from jax.sharding import PartitionSpec as P

NCH = 1024
NB = 128


def chol_solve(factor, rhs):
    first = lax.linalg.triangular_solve(factor, rhs, left_side=True, lower=True)
    return lax.linalg.triangular_solve(factor, first, left_side=True, lower=True, transpose_a=True)


def inner_products(left, right):
    return jnp.einsum("pkr,plr->kl", left, right, precision=lax.Precision.HIGHEST)


def body(trial_block, ham_blocks, partners, stored_at, precond_diag):
    n_chan = lax.axis_size("chan")
    ch_dev = trial_block.shape[0]
    vectors = trial_block.shape[1]
    ncoup = partners.shape[1]
    capacity = 2 * ch_dev * ncoup // n_chan
    stored_rows = jnp.take(stored_at, partners.reshape(-1))
    owner_dev = stored_rows // ch_dev
    local_row = stored_rows % ch_dev
    one_hot = (owner_dev[:, None] == jnp.arange(n_chan, dtype=jnp.int32)[None, :]).astype(jnp.int32)
    running = jnp.cumsum(one_hot, axis=0)
    order_rank = jnp.sum(running * one_hot, axis=1) - 1
    slot_index = owner_dev * capacity + order_rank
    wanted = (
        jnp.zeros((n_chan * capacity,), jnp.int32)
        .at[slot_index]
        .set(local_row)
        .reshape(n_chan, capacity)
    )
    asked = lax.all_to_all(wanted, "chan", split_axis=0, concat_axis=0, tiled=True)
    rounded = trial_block.astype(jnp.bfloat16)
    whole_rows = lax.all_gather(rounded, "rad", axis=2, tiled=True)
    served = whole_rows[asked]
    received = lax.all_to_all(served, "chan", split_axis=0, concat_axis=0, tiled=True)
    full_splines = received.shape[3]
    coupled = received.reshape(n_chan * capacity, vectors, full_splines)[slot_index]
    coupled = coupled.reshape(ch_dev, ncoup, vectors, full_splines)
    applied = lax.dot_general(
        coupled, ham_blocks, (((1, 3), (1, 3)), ((0,), (0,))), preferred_element_type=jnp.float32
    )
    total_rows = jnp.float32(NCH * NB)
    proj_a, proj_b = lax.psum(
        (inner_products(trial_block, applied), inner_products(trial_block, trial_block)),
        ("chan", "rad"),
    )
    factor = jnp.linalg.cholesky(proj_b)
    coefficients = chol_solve(factor, proj_a)
    ritz_values = jnp.diagonal(coefficients)
    residual = applied - jnp.einsum(
        "pkr,kl->plr", trial_block, coefficients, precision=lax.Precision.HIGHEST
    )
    correction = residual / precond_diag[:, None, :]
    correlation = lax.psum(inner_products(trial_block, correction), ("chan", "rad"))
    mixing = chol_solve(factor, correlation)
    projected = correction - jnp.einsum(
        "pkr,kl->plr", trial_block, mixing, precision=lax.Precision.HIGHEST
    )
    correlation_gram = lax.psum(inner_products(projected, projected), ("chan", "rad")) / total_rows
    gram_factor = jnp.linalg.cholesky(correlation_gram)
    local_splines = projected.shape[2]
    flat_rows = jnp.transpose(projected, (1, 0, 2)).reshape(vectors, -1)
    solved = lax.linalg.triangular_solve(gram_factor, flat_rows, left_side=True, lower=True)
    new_block = jnp.transpose(solved.reshape(vectors, ch_dev, local_splines), (1, 0, 2))
    return (new_block, ritz_values)


def solution(mesh):
    return jax.shard_map(
        body,
        mesh=mesh,
        in_specs=(
            P("chan", None, "rad"),
            P("chan", None, "rad", None),
            P("chan", None),
            P(),
            P("chan", "rad"),
        ),
        out_specs=(P("chan", None, "rad"), P()),
        check_vma=False,
    )
```

profile of v0, /device:TPU:1, one launch (start us, length us, event | category | flops | bytes accessed | tf_op | source)
XLA Modules:
  0.0 426.4 jit_solution(2646082566353192529)
XLA Ops:
  0.6 0.0 copy-start
  0.6 0.8 copy.36
  1.5 0.1 reshape.211
  1.5 0.1 reshape.212
  1.6 0.0 copy-start.1
  1.7 0.7 copy-done.1
  2.3 1.0 gather_fusion
  3.3 0.1 fusion.4
  3.4 0.0 copy-start.2
  3.4 0.2 reduce_window_sum.11
  3.6 0.2 select_reduce_fusion
  3.8 1.0 scatter_custom_fusion
  4.8 0.7 all_to_all.11
  5.5 19.3 %all-to-all-start = ((s32[64,1,4]{2,1,0:T(1,128)}), s32[64,1,4]{2,1,0:T(1,128)S(1)}, u32[]{:S(2)}, u32[]{:S(2)}) async-start(s32[64,1,4]{2,1,0:T(1,128)} %bitcast.4), calls=%async_computation | async-start | bytes 65536 | tf_op jit(solution)/shard_map/all_to_all | solution.py:38
  24.8 0.0 copy-done.2
  24.8 0.1 copy.35
  24.9 14.3 %all_gather.3 = bf16[16,16,128]{1,0,2:T(8,128)(2,1)S(1)} all-gather(bf16[16,16,16]{1,0,2:T(8,128)(2,1)S(1)} %copy.35), channel_id=1, replica_groups=mesh['chan'=64,'rad'=8] {'rad'}, dimensions={2}, use_global_device_ids=true | all-gather | bytes 73728 | tf_op jit(solution)/shard_map/all_gather | solution.py:40
  39.2 0.4 copy.39
  39.6 0.0 all-to-all-done
  39.6 0.1 reshape.230
  39.8 1.8 gather_fusion.1
  41.5 14.8 %all-to-all-start.1 = ((bf16[64,4,16,128]{3,2,1,0:T(8,128)(2,1)}), bf16[64,4,16,128]{3,2,1,0:T(8,128)(2,1)S(1)}, u32[]{:S(2)}, u32[]{:S(2)}) async-start(bf16[64,4,16,128]{3,2,1,0:T(8,128)(2,1)} %bitcast.6), calls=%async_computation.1 | async-start | bytes 2097152 | tf_op jit(solution)/shard_map/all_to_all | solution.py:42
  56.4 0.2 convolution_bitcast_fusion.5
  56.6 52.5 %all-to-all-done.1 = bf16[64,4,16,128]{3,2,1,0:T(8,128)(2,1)S(1)} async-done(((bf16[64,4,16,128]{3,2,1,0:T(8,128)(2,1)}), bf16[64,4,16,128]{3,2,1,0:T(8,128)(2,1)S(1)}, u32[]{:S(2)}, u32[]{:S(2)}) %all-to-all-start.1) | async-done | bytes 1048608 | tf_op jit(solution)/shard_map/all_to_all | solution.py:42
  109.2 0.7 gather_fusion.2
  109.9 0.0 copy-done
  109.9 0.3 fusion.27
  110.2 0.3 convolution_bitcast_fusion.4
  110.4 103.4 %all-reduce = (f32[16,16]{0,1:T(8,128)S(1)}, f32[16,16]{0,1:T(8,128)S(1)}) all-reduce(f32[16,16]{0,1:T(8,128)S(1)} %convolution_bitcast_fusion.4, f32[16,16]{0,1:T(8,128)S(1)} %convolution_bitcast_fusion.5), channel_id=1, replica_groups=mesh['chan'=64,'rad'=8] {'chan','rad'}, use_global_device_ids=true, to_apply=%region_6.8 | all-reduce | flops 512 | bytes 4096 | tf_op jit(solution)/shard_map/psum | solution.py:50
  213.8 0.1 copy.41
  213.9 1.5 cholesky.44
  215.4 0.6 compare_reduce_fusion.1
  216.0 0.6 fusion.5
  216.7 1.2 custom-call.17
  217.9 0.2 fusion.14
  218.1 0.1 fusion.16
  218.3 0.0 copy-start.3
  218.3 0.3 fusion.9
  218.6 0.4 copy-done.3
  219.0 0.3 convolution_bitcast_fusion.3
  219.3 99.6 %psum.30 = f32[16,16]{0,1:T(8,128)S(1)} all-reduce(f32[16,16]{0,1:T(8,128)S(1)} %convolution_bitcast_fusion.3), channel_id=1, replica_groups=mesh['chan'=64,'rad'=8] {'chan','rad'}, use_global_device_ids=true, to_apply=%region_7.11 | all-reduce | flops 256 | bytes 2048 | tf_op jit(solution)/shard_map/psum | solution.py:61
  318.9 0.2 fusion.11
  319.1 0.2 convolution_bitcast_fusion.2
  319.3 0.3 fusion.1
  319.6 0.3 convolution_bitcast_fusion.1
  319.8 99.4 %psum.31 = f32[16,16]{0,1:T(8,128)S(1)} all-reduce(f32[16,16]{0,1:T(8,128)S(1)} %convolution_bitcast_fusion.1), channel_id=1, replica_groups=mesh['chan'=64,'rad'=8] {'chan','rad'}, use_global_device_ids=true, to_apply=%region_8.12 | all-reduce | flops 256 | bytes 2048 | tf_op jit(solution)/shard_map/psum | solution.py:66
  419.2 0.1 copy.44
  419.2 1.5 cholesky.55
  420.7 0.6 compare_reduce_fusion
  421.4 0.6 fusion.6
  422.0 1.2 custom-call.11
  423.3 0.1 copy.45
  423.3 0.1 reshape.215
  423.4 0.1 copy.56
  423.5 1.2 gather_fusion.3
  424.7 1.7 convolution_bitcast_fusion
  (14 shorter events, 0.2 us)
Async XLA Ops:
  0.6 109.2 %copy-start = (bf16[16,8,16,128]{3,2,1,0:T(8,128)(2,1)S(1)}, bf16[16,8,16,128]{3,2,1,0:T(8,128)(2,1)}, u32[]{:S(2)}) copy-start(bf16[16,8,16,128]{3,2,1,0:T(8,128)(2,1)} %param.11) | copy-start | bytes 1572868
  1.6 0.7 copy-start.1
  3.4 21.4 %copy-start.2 = (f32[16,16,16]{2,1,0:T(8,128)S(1)}, f32[16,16,16]{2,1,0:T(8,128)}, u32[]{:S(2)}) copy-start(f32[16,16,16]{2,1,0:T(8,128)} %param.10) | copy-start | bytes 49156
  5.5 34.1 %all-to-all-start = ((s32[64,1,4]{2,1,0:T(1,128)}), s32[64,1,4]{2,1,0:T(1,128)S(1)}, u32[]{:S(2)}, u32[]{:S(2)}) async-start(s32[64,1,4]{2,1,0:T(1,128)} %bitcast.4), calls=%async_computation | async-start | bytes 65536 | tf_op jit(solution)/shard_map/all_to_all | solution.py:38
  41.5 67.6 %all-to-all-start.1 = ((bf16[64,4,16,128]{3,2,1,0:T(8,128)(2,1)}), bf16[64,4,16,128]{3,2,1,0:T(8,128)(2,1)S(1)}, u32[]{:S(2)}, u32[]{:S(2)}) async-start(bf16[64,4,16,128]{3,2,1,0:T(8,128)(2,1)} %bitcast.6), calls=%async_computation.1 | async-start | bytes 2097152 | tf_op jit(solution)/shard_map/all_to_all | solution.py:42
  218.3 0.7 copy-start.3
where the time goes:
time: 427 us; the launch traced here: 426 us
  blocking collectives  317 us (74%)
  waiting for transfers between devices  52.5 us (12%)
  starting transfers between devices  34.1 us (8%)
  local copies, waits for them, and re-layouts  9.41 us (2%)
  other arithmetic  8.53 us (2%)
  matrix products  4.37 us (1%)
    psum x1, blocking collectives, body(): lax.psum((inner_products(trial_block, applied), inner_products(trial_bloc...  103 us
    psum x1, blocking collectives, body(): lax.psum(inner_products(trial_block, correction), ('chan', 'rad'))  99.6 us
    psum x1, blocking collectives, body(): lax.psum(inner_products(projected, projected), ('chan', 'rad')) / total_rows  99.4 us
    all_to_all x1, waiting for transfers between devices, body(): lax.all_to_all(served, 'chan', split_axis=0, concat_axis=0, tiled=True)  52.5 us
    all_to_all x1, starting transfers between devices, body(): lax.all_to_all(wanted, 'chan', split_axis=0, concat_axis=0, tiled=True)  19.3 us
    all_to_all x1, starting transfers between devices, body(): lax.all_to_all(served, 'chan', split_axis=0, concat_axis=0, tiled=True)  14.8 us
    all_gather x1, blocking collectives, body(): whole_rows = lax.all_gather(rounded, 'rad', axis=2, tiled=True)  14.3 us
  transfers between devices with their start and end apart: 2, of which 1 were waited for; matrix products, arithmetic and copies ran while one was open for 0% of the time, Pallas kernels for 0%

commit v1 on v0

v1 whole, which is shorter than its diff:
```python
import jax
import jax.numpy as jnp
from jax import lax
from jax.experimental import pallas as pl
from jax.experimental.pallas import tpu as pltpu
from jax.sharding import PartitionSpec as P

MESH = pl.DeviceIdType.MESH
HI = lax.Precision.HIGHEST
F32 = jnp.float32
BF16 = jnp.bfloat16
TOTAL_ROWS = 1024.0 * 128.0
NJ = 8
CHUNK = 4


def kernel(t_ref, ham_ref, partners_ref, stored_ref, d_ref, new_ref, ritz_ref,
           hbuf, tbl, yall, red1, red2, red3,
           ham_sem, far_s, far_r, mid_s, mid_r, last_s, last_r, x_s, x_r, c_s, c_r, r1_s, r1_r, r2_s, r2_r, r3_s, r3_r):
    chan = lax.axis_index("chan")
    rad = lax.axis_index("rad")
    z, y = chan // 4, chan % 4
    zc, zf = z % 4, z // 4
    two = 2 - 4 * (z % 2)

    ham_copy = pltpu.make_async_copy(ham_ref, hbuf, ham_sem)
    ham_copy.start()

    def at(dz, yy):
        return (((z + dz + 16) % 16) * 4 + yy, rad)

    near = (0, 1, -1, two)
    barrier = pltpu.get_barrier_semaphore()
    met = 0
    for i in range(1, 8):
        pl.semaphore_signal(barrier, inc=1, device_id=(chan, rad ^ i), device_id_type=MESH)
        met += 1
    for m in range(1, 4):
        pl.semaphore_signal(barrier, inc=1, device_id=at(4 * m, y), device_id_type=MESH)
        met += 1
    for dy in range(4):
        for dz in (-2, -1, 0, 1, 2):
            if dy or dz:
                pl.semaphore_signal(barrier, inc=1, device_id=at(dz, y ^ dy), device_id_type=MESH)
                met += 1

    slot0 = y * 16 + zc * 4 + zf
    slot1 = zc * 16 + y * 4 + zf
    t2d = t_ref[...].reshape(256, 16)
    eye = (lax.broadcasted_iota(jnp.int32, (16, 16), 0) == lax.broadcasted_iota(jnp.int32, (16, 16), 1)).astype(BF16)
    turned = lax.dot_general(eye, t2d.astype(BF16), (((1,), (1,)), ((), ())), preferred_element_type=F32).astype(BF16)
    tbl[slot0] = turned[:, :128]
    tbl[64 + slot1] = turned[:, 128:]

    pl.semaphore_wait(barrier, met)

    def remote(src, dst, s, r, dev):
        copy = pltpu.make_async_remote_copy(src_ref=src, dst_ref=dst, send_sem=s, recv_sem=r,
                                            device_id=dev, device_id_type=MESH)
        copy.start()
        return copy

    far = []
    for m in range(1, 4):
        for h, slot in ((0, slot0), (1, 64 + slot1)):
            i = (m - 1) * 2 + h
            piece = tbl.at[pl.ds(slot, 1)]
            far.append(remote(piece, piece, far_s.at[i], far_r.at[i], at(4 * m, y)))

    t2 = jnp.concatenate([t_ref[p] for p in range(16)], axis=1)
    d2 = jnp.concatenate([d_ref[p:p + 1, :] for p in range(16)], axis=1)
    td = t2 / d2

    for c in far:
        c.wait_recv()
    mid = []
    for n in range(1, 4):
        piece = tbl.at[pl.ds(y * 16 + zc * 4, 4)]
        mid.append(remote(piece, piece, mid_s.at[n - 1], mid_r.at[n - 1], at(near[n], y)))
        piece = tbl.at[pl.ds(64 + zc * 16 + y * 4, 4)]
        mid.append(remote(piece, piece, mid_s.at[n + 2], mid_r.at[n + 2], at(0, y ^ n)))
    for c in mid:
        c.wait_recv()
    last = []
    for n in range(1, 4):
        piece = tbl.at[pl.ds(y * 16, 16)]
        last.append(remote(piece, piece, last_s.at[n - 1], last_r.at[n - 1], at(0, y ^ n)))
        piece = tbl.at[pl.ds(64 + zc * 16, 16)]
        last.append(remote(piece, piece, last_s.at[n + 2], last_r.at[n + 2], at(near[n], y)))
    for c in last:
        c.wait_recv()

    lane_group = lax.broadcasted_iota(jnp.int32, (16, 128), 1) // 16

    def select(j, carry):
        for hp in range(2):
            acc = jnp.zeros((16, 128), F32)
            for g in range(8):
                row = stored_ref[partners_ref[hp * 8 + g, j]]
                dev = row // 16
                rz, ry = dev // 4, dev % 4
                first = ry * 16 + (rz % 4) * 4 + rz // 4
                second = 64 + (rz % 4) * 16 + ry * 4 + rz // 4
                half = (row // 8) % 2
                tile = tbl[first + half * (second - first)].astype(F32)
                moved = pltpu.roll(tile, ((g - row % 8 + 8) % 8) * 16, 1)
                acc = jnp.where(lane_group == g, moved, acc)
            yall[j, rad, :, hp * 128:(hp + 1) * 128] = acc.astype(BF16)
        return carry

    other = (chan, rad ^ 1)
    along_x, across = [], []
    for c in range(NJ // CHUNK):
        lax.fori_loop(c * CHUNK, (c + 1) * CHUNK, select, 0)
        piece = yall.at[pl.ds(c * CHUNK, CHUNK), pl.ds(rad, 1)]
        for i in range(1, 4):
            k = c * 3 + i - 1
            along_x.append(remote(piece, piece, x_s.at[k], x_r.at[k], (chan, rad ^ (2 * i))))
        across.append(remote(piece, piece, c_s.at[c * 4], c_r.at[c * 4], other))

    ham_copy.wait()
    out_group = lax.broadcasted_iota(jnp.int32, (16, 256), 1) // 16
    applied_r = jnp.zeros((16, 256), F32)
    for c in range(NJ // CHUNK):
        for i in range(1, 4):
            along_x[c * 3 + i - 1].wait_recv()
            piece = yall.at[pl.ds(c * CHUNK, CHUNK), pl.ds(rad ^ (2 * i), 1)]
            across.append(remote(piece, piece, c_s.at[c * 4 + i], c_r.at[c * 4 + i], other))
    n_chunks = NJ // CHUNK
    for c in range(n_chunks):
        across[c].wait_recv()
        for i in range(3):
            across[n_chunks + c * 3 + i].wait_recv()
        js = range(c * CHUNK, (c + 1) * CHUNK)
        left = jnp.concatenate([hbuf[:, j].reshape(256, 128) for j in js], axis=1)
        right = yall[c * CHUNK:(c + 1) * CHUNK].reshape(CHUNK * 128, 256)
        out = jnp.dot(left, right, preferred_element_type=F32)
        for p in range(16):
            applied_r += jnp.where(out_group == p, out[p * 16:(p + 1) * 16, :], 0.0)

    turned_a = applied_r.T
    a2 = jnp.concatenate([turned_a[p * 16:(p + 1) * 16, :] for p in range(16)], axis=1)
    ad = a2 / d2

    left = jnp.concatenate([t2, td, ad], axis=0)
    right = jnp.concatenate([t2, a2, td, ad], axis=0)
    prods = lax.dot_general(left, right, (((1,), (1,)), ((), ())), precision=HI, preferred_element_type=F32)
    prods = jnp.concatenate([prods, jnp.zeros((48, 64), F32)], axis=1)
    lane = lax.broadcasted_iota(jnp.int32, (16, 128), 1)
    top = jnp.where(lane < 64, prods[:16], 0.0)
    second = jnp.where((lane >= 64) & (lane < 96), pltpu.roll(prods[16:32], 32, 1), 0.0)
    third = jnp.where((lane >= 96) & (lane < 112), pltpu.roll(prods[32:48], 48, 1), 0.0)
    mine = top + second + third

    red1[rad] = mine
    sums = []
    for i in range(1, 8):
        piece = red1.at[pl.ds(rad, 1)]
        sums.append(remote(piece, piece, r1_s.at[i - 1], r1_r.at[i - 1], (chan, rad ^ i)))
    for c in sums:
        c.wait_recv()
    total = red1[0]
    for i in range(1, 8):
        total = total + red1[i]

    red2[zf] = total
    for m in range(1, 4):
        piece = red2.at[pl.ds(zf, 1)]
        sums.append(remote(piece, piece, r2_s.at[m - 1], r2_r.at[m - 1], at(4 * m, y)))
    for c in sums[7:]:
        c.wait_recv()
    total = (red2[0] + red2[1]) + (red2[2] + red2[3])

    red3[y * 4 + zc] = total
    for dy in range(4):
        for n in range(4):
            if dy or n:
                i = dy * 4 + n - 1
                piece = red3.at[pl.ds(y * 4 + zc, 1)]
                sums.append(remote(piece, piece, r3_s.at[i], r3_r.at[i], at(near[n], y ^ dy)))
    for c in sums[10:]:
        c.wait_recv()
    total = red3[0]
    for i in range(1, 16):
        total = total + red3[i]

    rows = lax.broadcasted_iota(jnp.int32, (16, 128), 0)

    def block(m, b):
        return (pltpu.roll(m, 128 - 16 * b, 1) if b else m)[:, :16]

    m = total
    for i in range(16):
        pivot_row = m[i:i + 1, :] / m[i:i + 1, i:i + 1]
        m = jnp.where(rows == i, pivot_row, m - m[:, i:i + 1] * pivot_row)
    coef = block(m, 1)
    q_ta = block(total, 5)
    level = jnp.dot(jnp.concatenate([block(total, 2), block(m, 2), block(total, 4)], axis=0), coef,
                    precision=HI, preferred_element_type=F32)
    corr = block(total, 3) - level[:16]
    mixing = block(m, 3) - level[16:32]
    inner = level[32:48] - q_ta
    tn = (((0,), (0,)), ((), ()))
    gram = block(total, 6) + lax.dot_general(jnp.concatenate([-q_ta, coef, -corr], axis=0),
                                             jnp.concatenate([coef, inner, mixing], axis=0), tn,
                                             precision=HI, preferred_element_type=F32)
    gram = gram / TOTAL_ROWS
    projected = ad - lax.dot_general(jnp.concatenate([coef, mixing], axis=0), jnp.concatenate([td, t2], axis=0), tn,
                                     precision=HI, preferred_element_type=F32)
    small = (16, 16)
    diagonal = lax.broadcasted_iota(jnp.int32, small, 0) == lax.broadcasted_iota(jnp.int32, small, 1)
    ritz_ref[...] = jnp.sum(jnp.where(diagonal, coef, 0.0), axis=0, keepdims=True)

    e = jnp.concatenate([gram, jnp.where(diagonal, 1.0, 0.0), jnp.zeros((16, 96), F32)], axis=1)
    for i in range(15):
        e = e - jnp.where(rows > i, e[:, i:i + 1] / e[i:i + 1, i:i + 1], 0.0) * e[i:i + 1, :]
    pivots = jnp.sum(jnp.where(rows == lane, e, 0.0), axis=1, keepdims=True)
    inv_factor = block(e * lax.rsqrt(pivots), 1)
    new = jnp.dot(inv_factor, projected, precision=HI, preferred_element_type=F32)
    for p in range(16):
        half = new[:, (p // 8) * 128:(p // 8 + 1) * 128]
        g = p % 8
        new_ref[p] = (pltpu.roll(half, 128 - 16 * g, 1) if g else half)[:, :16]

    for c in far + mid + last + along_x + across + sums:
        c.wait_send()


def body(trial_block, ham_blocks, partners, stored_at, precond_diag):
    vmem = pl.BlockSpec(memory_space=pltpu.VMEM)
    smem = pl.BlockSpec(memory_space=pltpu.SMEM)
    dma = pltpu.SemaphoreType.DMA
    n_chunks = NJ // CHUNK
    counts = (6, 6, 6, 6, 6, 6, 3 * n_chunks, 3 * n_chunks, 4 * n_chunks, 4 * n_chunks, 7, 7, 3, 3, 15, 15)
    new_block, ritz = pl.pallas_call(
        kernel,
        out_shape=(jax.ShapeDtypeStruct((16, 16, 16), F32), jax.ShapeDtypeStruct((1, 16), F32)),
        in_specs=[vmem, pl.BlockSpec(memory_space=pl.ANY), smem, smem, vmem],
        out_specs=(vmem, vmem),
        scratch_shapes=[
            pltpu.VMEM((16, 8, 16, 128), BF16),
            pltpu.VMEM((128, 16, 128), BF16),
            pltpu.VMEM((8, 8, 16, 256), BF16),
            pltpu.VMEM((8, 16, 128), F32),
            pltpu.VMEM((4, 16, 128), F32),
            pltpu.VMEM((16, 16, 128), F32),
            dma,
            *[dma((n,)) for n in counts],
        ],
        compiler_params=pltpu.CompilerParams(collective_id=0, has_side_effects=True, vmem_limit_bytes=32 * 2**20),
    )(trial_block, ham_blocks, partners, stored_at, precond_diag)
    return new_block, ritz.reshape(16)


def solution(mesh):
    return jax.shard_map(
        body,
        mesh=mesh,
        in_specs=(
            P("chan", None, "rad"),
            P("chan", None, "rad", None),
            P("chan", None),
            P(),
            P("chan", "rad"),
        ),
        out_specs=(P("chan", None, "rad"), P()),
        check_vma=False,
    )
```

time: 427 us -> 66 us (0.15)
  blocking collectives: 317 us -> 0 us
  Pallas kernels: 0 us -> 61 us
  waiting for transfers between devices: 52.5 us -> 0 us
  starting transfers between devices: 34.1 us -> 0 us
  other arithmetic: 8.53 us -> 0 us
  local copies, waits for them, and re-layouts: 9.41 us -> 3.89 us
  matrix products: 4.37 us -> 0 us
    psum x3 -> x0, blocking collectives: 302 us -> none  [the longest x1 103 us: body(): lax.psum((inner_products(trial_block, applied), inner_products(trial_bloc...]
    pallas_call x0 -> x1, Pallas kernels: none -> 61 us  [body(): pl.pallas_call(kernel, out_shape=(jax.ShapeDtypeStruct((16, 16, 16), F32)...]
    all_to_all x2 -> x0, waiting for transfers between devices: 52.5 us -> none  [the longest x1 52.5 us: body(): lax.all_to_all(served, 'chan', split_axis=0, concat_axis=0, tiled=True)]
    all_to_all x2 -> x0, starting transfers between devices: 34.1 us -> none  [the longest x1 19.3 us: body(): lax.all_to_all(wanted, 'chan', split_axis=0, concat_axis=0, tiled=True)]
    all_gather x1 -> x0, blocking collectives: 14.3 us -> none  [body(): whole_rows = lax.all_gather(rounded, 'rad', axis=2, tiled=True)]
    another operation x11 -> x0, other arithmetic: 8.18 us -> none  [the longest x3 2.13 us: body(): gram_factor = jnp.linalg.cholesky(correlation_gram)]
    gather x4 -> x0, local copies, waits for them, and re-layouts: 4.63 us -> none  [the longest x1 1.78 us: body(): served = whole_rows[asked]]
  transfers between devices with their start and end apart: 2 -> 0, of which waited for: 1 -> 0; matrix products, arithmetic and copies ran while one was open for 0% -> 0% of each run, Pallas kernels for 0% -> 0%
where the time goes in v1:
time: 66 us; the launch traced here: 65.5 us
  Pallas kernels  61 us (92%)
  local copies, waits for them, and re-layouts  3.89 us (6%)
  between operations  0.66 us (1%)
    pallas_call x1, Pallas kernels, body(): pl.pallas_call(kernel, out_shape=(jax.ShapeDtypeStruct((16, 16, 16), F32)...  61 us
    unnamed x11, local copies, waits for them, and re-layouts  3.89 us

profile of v1, /device:TPU:1, one launch (start us, length us, event | category | flops | bytes accessed | tf_op | source)
XLA Modules:
  0.0 65.5 jit_solution(12826489235888983299)
XLA Ops:
  0.6 0.0 copy-start.2
  0.6 0.0 copy-start.3
  0.7 0.8 %copy.7.partners_ref = s32[16,8]{1,0:T(8,128)S(1)} copy(s32[16,8]{0,1:T(8,128)} %param.7) | data formatting | bytes 1024 | tf_op args[2]
  1.4 0.0 copy-done.2
  1.4 0.0 copy-done.3
  1.4 0.0 copy-start
  1.4 1.0 %copy-done = bf16[16,8,16,128]{3,2,1,0:T(8,128)(2,1)S(1)} copy-done((bf16[16,8,16,128]{3,2,1,0:T(8,128)(2,1)S(1)}, bf16[16,8,16,128]{3,2,1,0:T(8,128)(2,1)}, u32[]{:S(2)}) %copy-start) | copy-done | bytes 524312
  2.5 0.0 copy-start.1
  2.5 0.9 %copy-done.1 = f32[16,16,16]{2,1,0:T(8,128)S(1)} copy-done((f32[16,16,16]{2,1,0:T(8,128)S(1)}, f32[16,16,16]{2,1,0:T(8,128)}, u32[]{:S(2)}) %copy-start.1) | copy-done | bytes 16408
  3.4 61.0 %shard_map.68 = (f32[16,16,16]{2,1,0:T(8,128)S(1)}, f32[1,16]{1,0:T(1,128)S(1)}) custom-call(f32[16,16,16]{2,1,0:T(8,128)S(1)} %copy-done.1, bf16[16,8,16,128]{3,2,1,0:T(8,128)(2,1)S(1)} %copy-done, s32[16,8]{1,0:T(8,128)S(1)} %copy.7.partners_ref, s32[1024]{0:T(1024)S(1)} %copy-done.3, f32[16,16]{1,0:T(8,128)S(1)} %copy-done.2), custom_call_target="tpu_custom_call" | custom-call | tf_op jit(solution)/shard_map/pallas_call | solution.py:235
  64.4 0.7 %copy.10 = f32[16,16,16]{2,1,0:T(8,128)} copy(f32[16,16,16]{2,1,0:T(8,128)S(1)} %get-tuple-element.8) | data formatting | bytes 32768
  65.0 0.5 copy.11
Async XLA Ops:
  0.6 0.8 %copy-start.2 = (f32[16,16]{1,0:T(8,128)S(1)}, f32[16,16]{1,0:T(8,128)}, u32[]{:S(2)}) copy-start(f32[16,16]{1,0:T(8,128)} %d_ref.1) | copy-start | bytes 3076
  0.6 0.8 %copy-start.3 = (s32[1024]{0:T(1024)S(1)}, s32[1024]{0:T(1024)}, u32[]{:S(2)}) copy-start(s32[1024]{0:T(1024)} %stored_ref.1) | copy-start | bytes 12292
  1.4 1.0 %copy-start = (bf16[16,8,16,128]{3,2,1,0:T(8,128)(2,1)S(1)}, bf16[16,8,16,128]{3,2,1,0:T(8,128)(2,1)}, u32[]{:S(2)}) copy-start(bf16[16,8,16,128]{3,2,1,0:T(8,128)(2,1)} %ham_ref.1) | copy-start | bytes 1572868
  2.5 0.9 %copy-start.1 = (f32[16,16,16]{2,1,0:T(8,128)S(1)}, f32[16,16,16]{2,1,0:T(8,128)}, u32[]{:S(2)}) copy-start(f32[16,16,16]{2,1,0:T(8,128)} %t_ref.1) | copy-start | bytes 49156

commit v2 on v1

--- a/solution.py
+++ b/solution.py
@@ -11,31 +11,27 @@
 BF16 = jnp.bfloat16
 TOTAL_ROWS = 1024.0 * 128.0
 NJ = 8
-CHUNK = 4
-
-
-def kernel(t_ref, ham_ref, partners_ref, stored_ref, d_ref, new_ref, ritz_ref,
-           hbuf, tbl, yall, red1, red2, red3,
-           ham_sem, far_s, far_r, mid_s, mid_r, last_s, last_r, x_s, x_r, c_s, c_r, r1_s, r1_r, r2_s, r2_r, r3_s, r3_r):
+CHUNK = 2
+
+
+def kernel(t_hbm, ham_hbm, partners_hbm, stored_hbm, d_hbm, new_ref, ritz_ref,
+           t_ref, d_ref, hbuf, partners_ref, stored_ref, place, tbl, yall, red1, red2, red3,
+           in_sem, far_s, far_r, own_s, own_r, fwd_s, fwd_r, x_s, x_r, c_s, c_r, r1_s, r1_r, r2_s, r2_r, r3_s, r3_r):
     chan = lax.axis_index("chan")
     rad = lax.axis_index("rad")
     z, y = chan // 4, chan % 4
     zc, zf = z % 4, z // 4
     two = 2 - 4 * (z % 2)
 
-    ham_copy = pltpu.make_async_copy(ham_ref, hbuf, ham_sem)
-    ham_copy.start()
-
     def at(dz, yy):
         return (((z + dz + 16) % 16) * 4 + yy, rad)
 
+    t_copy = pltpu.make_async_copy(t_hbm, t_ref, in_sem.at[0])
+    t_copy.start()
     near = (0, 1, -1, two)
     barrier = pltpu.get_barrier_semaphore()
     met = 0
-    for i in range(1, 8):
-        pl.semaphore_signal(barrier, inc=1, device_id=(chan, rad ^ i), device_id_type=MESH)
-        met += 1
-    for m in range(1, 4):
+    for m in (2, 1, 3):
         pl.semaphore_signal(barrier, inc=1, device_id=at(4 * m, y), device_id_type=MESH)
         met += 1
     for dy in range(4):
@@ -43,14 +39,22 @@
             if dy or dz:
                 pl.semaphore_signal(barrier, inc=1, device_id=at(dz, y ^ dy), device_id_type=MESH)
                 met += 1
+    for i in range(1, 8):
+        pl.semaphore_signal(barrier, inc=1, device_id=(chan, rad ^ i), device_id_type=MESH)
+        met += 1
+    rest = [pltpu.make_async_copy(src, dst, in_sem.at[i + 1]) for i, (src, dst) in enumerate(
+        ((d_hbm, d_ref), (partners_hbm, partners_ref), (stored_hbm, stored_ref), (ham_hbm, hbuf)))]
+    for c in rest:
+        c.start()
 
     slot0 = y * 16 + zc * 4 + zf
-    slot1 = zc * 16 + y * 4 + zf
+    slot1 = 64 + zc * 16 + y * 4 + zf
+    t_copy.wait()
     t2d = t_ref[...].reshape(256, 16)
     eye = (lax.broadcasted_iota(jnp.int32, (16, 16), 0) == lax.broadcasted_iota(jnp.int32, (16, 16), 1)).astype(BF16)
     turned = lax.dot_general(eye, t2d.astype(BF16), (((1,), (1,)), ((), ())), preferred_element_type=F32).astype(BF16)
     tbl[slot0] = turned[:, :128]
-    tbl[64 + slot1] = turned[:, 128:]
+    tbl[slot1] = turned[:, 128:]
 
     pl.semaphore_wait(barrier, met)
 
@@ -61,33 +65,62 @@
         return copy
 
     far = []
-    for m in range(1, 4):
-        for h, slot in ((0, slot0), (1, 64 + slot1)):
+    for m in (2, 1, 3):
+        for h, slot in ((0, slot0), (1, slot1)):
             i = (m - 1) * 2 + h
             piece = tbl.at[pl.ds(slot, 1)]
             far.append(remote(piece, piece, far_s.at[i], far_r.at[i], at(4 * m, y)))
 
+    for c in rest:
+        c.wait()
     t2 = jnp.concatenate([t_ref[p] for p in range(16)], axis=1)
     d2 = jnp.concatenate([d_ref[p:p + 1, :] for p in range(16)], axis=1)
     td = t2 / d2
 
+    def locate(j, carry):
+        for p in range(16):
+            row = stored_ref[partners_ref[j, p]]
+            ry, rc, rf = (row // 16) % 4, (row // 64) % 4, row // 256
+            half = (row // 8) % 2
+            place[j * 16 + p] = half * (64 + rc * 16 + ry * 4) + (1 - half) * (ry * 16 + rc * 4) + rf
+            place[128 + j * 16 + p] = ((p - row + 16) % 8) * 16
+        return carry
+
+    lax.fori_loop(0, NJ, locate, 0)
+
     for c in far:
         c.wait_recv()
-    mid = []
-    for n in range(1, 4):
-        piece = tbl.at[pl.ds(y * 16 + zc * 4, 4)]
-        mid.append(remote(piece, piece, mid_s.at[n - 1], mid_r.at[n - 1], at(near[n], y)))
-        piece = tbl.at[pl.ds(64 + zc * 16 + y * 4, 4)]
-        mid.append(remote(piece, piece, mid_s.at[n + 2], mid_r.at[n + 2], at(0, y ^ n)))
-    for c in mid:
-        c.wait_recv()
-    last = []
-    for n in range(1, 4):
-        piece = tbl.at[pl.ds(y * 16, 16)]
-        last.append(remote(piece, piece, last_s.at[n - 1], last_r.at[n - 1], at(0, y ^ n)))
-        piece = tbl.at[pl.ds(64 + zc * 16, 16)]
-        last.append(remote(piece, piece, last_s.at[n + 2], last_r.at[n + 2], at(near[n], y)))
-    for c in last:
+    sent = []
+
+    def hand_on(h, first, group, k, sems):
+        piece = tbl.at[pl.ds(first, 4)]
+        to = at(near[k], y) if group == "z" else at(0, y ^ k)
+        s, r, i = sems
+        copy = remote(piece, piece, s.at[i], r.at[i], to)
+        sent.append(copy)
+        return copy
+
+    own0, own1 = y * 16 + zc * 4, 64 + zc * 16 + y * 4
+    first_z, first_y, second_z, second_y = {}, {}, {}, {}
+    for k in (3, 1, 2):
+        first_z[k] = hand_on(0, own0, "z", k, (own_s, own_r, k - 1))
+    for k in (2, 1, 3):
+        second_y[k] = hand_on(1, own1, "y", k, (own_s, own_r, 3 + k - 1))
+    for k in (2, 1, 3):
+        first_y[k] = hand_on(0, own0, "y", k, (own_s, own_r, 6 + k - 1))
+    for k in (3, 1, 2):
+        second_z[k] = hand_on(1, own1, "z", k, (own_s, own_r, 9 + k - 1))
+    onward = []
+    for n, d in ((1, 1), (2, 3), (3, 2)):
+        first_z[n].wait_recv()
+        came = y * 16 + ((z - near[n] + 16) % 4) * 4
+        for k in (2, 1, 3):
+            onward.append(hand_on(0, came, "y", k, (fwd_s, fwd_r, (n - 1) * 3 + k - 1)))
+        second_y[d].wait_recv()
+        came = 64 + zc * 16 + (y ^ d) * 4
+        for k in (3, 1, 2):
+            onward.append(hand_on(1, came, "z", k, (fwd_s, fwd_r, 9 + (d - 1) * 3 + k - 1)))
+    for c in [*first_y.values(), *second_z.values(), *onward]:
         c.wait_recv()
 
     lane_group = lax.broadcasted_iota(jnp.int32, (16, 128), 1) // 16
@@ -96,47 +129,40 @@
         for hp in range(2):
             acc = jnp.zeros((16, 128), F32)
             for g in range(8):
-                row = stored_ref[partners_ref[hp * 8 + g, j]]
-                dev = row // 16
-                rz, ry = dev // 4, dev % 4
-                first = ry * 16 + (rz % 4) * 4 + rz // 4
-                second = 64 + (rz % 4) * 16 + ry * 4 + rz // 4
-                half = (row // 8) % 2
-                tile = tbl[first + half * (second - first)].astype(F32)
-                moved = pltpu.roll(tile, ((g - row % 8 + 8) % 8) * 16, 1)
+                i = j * 16 + hp * 8 + g
+                moved = pltpu.roll(tbl[place[i]].astype(F32), place[128 + i], 1)
                 acc = jnp.where(lane_group == g, moved, acc)
             yall[j, rad, :, hp * 128:(hp + 1) * 128] = acc.astype(BF16)
         return carry
 
     other = (chan, rad ^ 1)
-    along_x, across = [], []
-    for c in range(NJ // CHUNK):
+    along_x, across = {}, {}
+    n_chunks = NJ // CHUNK
+    for c in range(n_chunks):
         lax.fori_loop(c * CHUNK, (c + 1) * CHUNK, select, 0)
         piece = yall.at[pl.ds(c * CHUNK, CHUNK), pl.ds(rad, 1)]
-        for i in range(1, 4):
+        for i in (2, 1, 3):
             k = c * 3 + i - 1
-            along_x.append(remote(piece, piece, x_s.at[k], x_r.at[k], (chan, rad ^ (2 * i))))
-        across.append(remote(piece, piece, c_s.at[c * 4], c_r.at[c * 4], other))
-
-    ham_copy.wait()
+            along_x[c, i] = remote(piece, piece, x_s.at[k], x_r.at[k], (chan, rad ^ (2 * i)))
+        across[c, 0] = remote(piece, piece, c_s.at[c * 4], c_r.at[c * 4], other)
+
     out_group = lax.broadcasted_iota(jnp.int32, (16, 256), 1) // 16
     applied_r = jnp.zeros((16, 256), F32)
-    for c in range(NJ // CHUNK):
-        for i in range(1, 4):
-            along_x[c * 3 + i - 1].wait_recv()
-            piece = yall.at[pl.ds(c * CHUNK, CHUNK), pl.ds(rad ^ (2 * i), 1)]
-            across.append(remote(piece, piece, c_s.at[c * 4 + i], c_r.at[c * 4 + i], other))
-    n_chunks = NJ // CHUNK
-    for c in range(n_chunks):
-        across[c].wait_recv()
-        for i in range(3):
-            across[n_chunks + c * 3 + i].wait_recv()
-        js = range(c * CHUNK, (c + 1) * CHUNK)
-        left = jnp.concatenate([hbuf[:, j].reshape(256, 128) for j in js], axis=1)
-        right = yall[c * CHUNK:(c + 1) * CHUNK].reshape(CHUNK * 128, 256)
-        out = jnp.dot(left, right, preferred_element_type=F32)
-        for p in range(16):
-            applied_r += jnp.where(out_group == p, out[p * 16:(p + 1) * 16, :], 0.0)
+    for c in range(n_chunks + 1):
+        if c < n_chunks:
+            for i in (1, 3, 2):
+                along_x[c, i].wait_recv()
+                piece = yall.at[pl.ds(c * CHUNK, CHUNK), pl.ds(rad ^ (2 * i), 1)]
+                across[c, i] = remote(piece, piece, c_s.at[c * 4 + i], c_r.at[c * 4 + i], other)
+        if c:
+            for i in range(4):
+                across[c - 1, i].wait_recv()
+            js = range((c - 1) * CHUNK, c * CHUNK)
+            left = jnp.concatenate([hbuf[:, j].reshape(256, 128) for j in js], axis=1)
+            right = yall[(c - 1) * CHUNK:c * CHUNK].reshape(CHUNK * 128, 256)
+            out = jnp.dot(left, right, preferred_element_type=F32)
+            for p in range(16):
+                applied_r += jnp.where(out_group == p, out[p * 16:(p + 1) * 16, :], 0.0)
 
     turned_a = applied_r.T
     a2 = jnp.concatenate([turned_a[p * 16:(p + 1) * 16, :] for p in range(16)], axis=1)
@@ -222,33 +248,37 @@
         g = p % 8
         new_ref[p] = (pltpu.roll(half, 128 - 16 * g, 1) if g else half)[:, :16]
 
-    for c in far + mid + last + along_x + across + sums:
+    for c in [*far, *sent, *along_x.values(), *across.values(), *sums]:
         c.wait_send()
 
 
 def body(trial_block, ham_blocks, partners, stored_at, precond_diag):
     vmem = pl.BlockSpec(memory_space=pltpu.VMEM)
-    smem = pl.BlockSpec(memory_space=pltpu.SMEM)
+    hbm = pl.BlockSpec(memory_space=pltpu.HBM)
     dma = pltpu.SemaphoreType.DMA
     n_chunks = NJ // CHUNK
-    counts = (6, 6, 6, 6, 6, 6, 3 * n_chunks, 3 * n_chunks, 4 * n_chunks, 4 * n_chunks, 7, 7, 3, 3, 15, 15)
+    counts = (5, 6, 6, 12, 12, 18, 18, 3 * n_chunks, 3 * n_chunks, 4 * n_chunks, 4 * n_chunks, 7, 7, 3, 3, 15, 15)
     new_block, ritz = pl.pallas_call(
         kernel,
         out_shape=(jax.ShapeDtypeStruct((16, 16, 16), F32), jax.ShapeDtypeStruct((1, 16), F32)),
-        in_specs=[vmem, pl.BlockSpec(memory_space=pl.ANY), smem, smem, vmem],
+        in_specs=[hbm] * 5,
         out_specs=(vmem, vmem),
         scratch_shapes=[
+            pltpu.VMEM((16, 16, 16), F32),
+            pltpu.VMEM((16, 16), F32),
             pltpu.VMEM((16, 8, 16, 128), BF16),
+            pltpu.SMEM((8, 16), jnp.int32),
+            pltpu.SMEM((1024,), jnp.int32),
+            pltpu.SMEM((256,), jnp.int32),
             pltpu.VMEM((128, 16, 128), BF16),
             pltpu.VMEM((8, 8, 16, 256), BF16),
             pltpu.VMEM((8, 16, 128), F32),
             pltpu.VMEM((4, 16, 128), F32),
             pltpu.VMEM((16, 16, 128), F32),
-            dma,
             *[dma((n,)) for n in counts],
         ],
-        compiler_params=pltpu.CompilerParams(collective_id=0, has_side_effects=True, vmem_limit_bytes=32 * 2**20),
-    )(trial_block, ham_blocks, partners, stored_at, precond_diag)
+        compiler_params=pltpu.CompilerParams(collective_id=0, has_side_effects=True, vmem_limit_bytes=60 * 2**20),
+    )(trial_block, ham_blocks, partners.T, stored_at, precond_diag)
     return new_block, ritz.reshape(16)
 
 

time: 66 us -> 62 us (0.939)
  local copies, waits for them, and re-layouts: 3.89 us -> 2.08 us
  Pallas kernels: 61 us -> 59.2 us
    pallas_call x1, Pallas kernels: 61 us -> 59.2 us  [body(): pl.pallas_call(kernel, out_shape=(jax.ShapeDtypeStruct((16, 16, 16), F32)...]
    unnamed x11 -> x4, local copies, waits for them, and re-layouts: 3.89 us -> 2.08 us
where the time goes in v2:
time: 62 us; the launch traced here: 61.9 us
  Pallas kernels  59.2 us (95%)
  local copies, waits for them, and re-layouts  2.08 us (3%)
  between operations  0.65 us (1%)
    pallas_call x1, Pallas kernels, body(): pl.pallas_call(kernel, out_shape=(jax.ShapeDtypeStruct((16, 16, 16), F32)...  59.2 us
    unnamed x4, local copies, waits for them, and re-layouts  2.08 us

profile of v2, /device:TPU:1, one launch (start us, length us, event | category | flops | bytes accessed | tf_op | source)
XLA Modules:
  0.0 61.9 jit_solution(13186098786233418414)
XLA Ops:
  0.6 59.2 %shard_map.68 = (f32[16,16,16]{2,1,0:T(8,128)}, f32[1,16]{1,0:T(1,128)}) custom-call(f32[16,16,16]{2,1,0:T(8,128)} %t_hbm.1, bf16[16,8,16,128]{3,2,1,0:T(8,128)(2,1)} %ham_hbm.1, s32[8,16]{1,0:T(8,128)} %bitcast.2, s32[1024]{0:T(1024)} %stored_hbm.1, f32[16,16]{1,0:T(8,128)} %d_hbm.1), custom_call_target="tpu_custom_call" | custom-call | tf_op jit(solution)/shard_map/pallas_call | solution.py:261
  59.8 0.0 copy-start
  59.8 1.6 %copy.9 = f32[16,16,16]{2,1,0:T(8,128)} copy(f32[16,16,16]{2,1,0:T(8,128)} %get-tuple-element.8) | data formatting | bytes 32768
  61.4 0.0 copy-done
  61.4 0.5 copy.10
Async XLA Ops:
  59.8 1.6 %copy-start = (f32[1,16]{1,0:T(1,128)S(1)}, f32[1,16]{1,0:T(1,128)}, u32[]{:S(2)}) copy-start(f32[1,16]{1,0:T(1,128)} %get-tuple-element.5) | copy-start | bytes 196

commit v3 on v2

v3 whole, which is shorter than its diff:
```python
import functools

import jax
import jax.numpy as jnp
from jax import lax
from jax.experimental import pallas as pl
from jax.experimental.pallas import tpu as pltpu
from jax.sharding import PartitionSpec as P

MESH = pl.DeviceIdType.MESH
HI = lax.Precision.HIGHEST
F32 = jnp.float32
BF16 = jnp.bfloat16
TOTAL_ROWS = 1024.0 * 128.0
NJ = 8
ALONG_Z = (8, 7, 9, 6, 10, 5, 11, 4, 12, 3, 13, 2, 14, 1, 15)
IN_PLANE = sorted(((dy, dr) for dy in range(4) for dr in range(8) if dy or dr),
                  key=lambda d: -((0, 1, 2, 1)[d[0]] + (0, 1, 2, 1)[d[1] // 2]))
GROUPS = ((0, 4), (4, 8), (8, 12), (12, 16))
CHUNK = 4


def by_distance(d):
    return 2 * d - 1 if 0 < d <= 8 else 2 * (16 - d) % 32


def kernel(t_hbm, ham_hbm, partners_hbm, stored_hbm, d_hbm, new_ref, ritz_ref,
           t_ref, d_ref, hbuf, partners_ref, stored_ref, place, tbl, yall, trial1, trial2, red1, red2,
           in_sem, far_s, far_r, own_s, own_r, x_s, x_r, c_s, c_r,
           t1_s, t1_r, t2_s, t2_r, r1_s, r1_r, r2_s, r2_r):
    chan = lax.axis_index("chan")
    rad = lax.axis_index("rad")
    z, y = chan // 4, chan % 4

    def at(dz, yy):
        return (((z + dz + 16) % 16) * 4 + yy, rad)

    t_copy = pltpu.make_async_copy(t_hbm, t_ref, in_sem.at[0])
    t_copy.start()
    barrier = pltpu.get_barrier_semaphore()
    for m in ALONG_Z:
        pl.semaphore_signal(barrier, inc=1, device_id=at(m, y), device_id_type=MESH)
    for dy, dr in IN_PLANE:
        pl.semaphore_signal(barrier, inc=1, device_id=(z * 4 + (y ^ dy), rad ^ dr), device_id_type=MESH)
    rest = [pltpu.make_async_copy(src, dst, in_sem.at[i + 1]) for i, (src, dst) in enumerate(
        ((d_hbm, d_ref), (partners_hbm, partners_ref), (stored_hbm, stored_ref), (ham_hbm, hbuf)))]
    for c in rest:
        c.start()

    t_copy.wait()
    t2d = t_ref[...].reshape(256, 16)
    eye = (lax.broadcasted_iota(jnp.int32, (16, 16), 0) == lax.broadcasted_iota(jnp.int32, (16, 16), 1)).astype(BF16)
    turned = lax.dot_general(eye, t2d.astype(BF16), (((1,), (1,)), ((), ())), preferred_element_type=F32).astype(BF16)
    tbl[y * 16, 0] = turned[:, :128]
    tbl[y * 16, 1] = turned[:, 128:]

    pl.semaphore_wait(barrier, len(ALONG_Z) + len(IN_PLANE))

    def remote(src, dst, s, r, dev):
        copy = pltpu.make_async_remote_copy(src_ref=src, dst_ref=dst, send_sem=s, recv_sem=r,
                                            device_id=dev, device_id_type=MESH)
        copy.start()
        return copy

    far = {}
    for m in ALONG_Z:
        far[by_distance(16 - m)] = remote(tbl.at[pl.ds(y * 16, 1)], tbl.at[pl.ds(y * 16 + by_distance(16 - m), 1)],
                                          far_s.at[m], far_r.at[m], at(m, y))

    for c in rest:
        c.wait()
    t2 = jnp.concatenate([t_ref[p] for p in range(16)], axis=1)
    d2 = jnp.concatenate([d_ref[p:p + 1, :] for p in range(16)], axis=1)
    td = t2 / d2

    def pack(m):
        left_half = lax.broadcasted_iota(jnp.int32, (8, 128), 1) < 64
        return jnp.where(left_half, m[:8], pltpu.roll(m[8:], 64, 1))

    def unpack(m):
        return jnp.concatenate([m, pltpu.roll(m, 64, 1)], axis=0)

    def widen(m):
        return jnp.concatenate([m, jnp.zeros((m.shape[0], 128 - m.shape[1]), F32)], axis=1)

    sums = []

    def to_plane(buf, s, r):
        piece = buf.at[pl.ds(y * 8 + rad, 1)]
        return [remote(piece, piece, s.at[i], r.at[i], (z * 4 + (y ^ dy), rad ^ dr))
                for i, (dy, dr) in enumerate(IN_PLANE)]

    def to_planes(buf, s, r):
        piece = buf.at[pl.ds(z, 1)]
        return [remote(piece, piece, s.at[m], r.at[m], at(m, y)) for m in ALONG_Z]

    def summed(buf, copies):
        for c in copies:
            c.wait_recv()
        sums.extend(copies)
        parts = [buf[i] for i in range(buf.shape[0])]
        while len(parts) > 1:
            parts = [u + v for u, v in zip(parts[::2], parts[1::2])]
        return parts[0]

    lane = lax.broadcasted_iota(jnp.int32, (16, 128), 1)
    nt = (((1,), (1,)), ((), ()))

    both = jnp.concatenate([t2, td], axis=0)
    prods = widen(lax.dot_general(both, both, nt, precision=HI, preferred_element_type=F32))
    prods = jnp.where(lane < 32, prods[:16], jnp.where(lane < 48, pltpu.roll(prods[16:], 16, 1), 0.0))
    trial1[y * 8 + rad] = pack(prods)
    trial_copies = to_plane(trial1, t1_s, t1_r)

    def locate(j, carry):
        for p in range(16):
            row = stored_ref[partners_ref[j, p]]
            ahead = (row // 64 - z + 16) % 16
            order = jnp.where(ahead > 8, 32 - 2 * ahead, jnp.maximum(2 * ahead - 1, 0))
            place[j * 16 + p] = ((row // 16) % 4 * 16 + order) * 2 + (row // 8) % 2
            place[128 + j * 16 + p] = ((p - row + 16) % 8) * 16
        return carry

    lax.fori_loop(0, NJ, locate, 0)

    sent = []
    for g, (first, end) in enumerate(GROUPS):
        for i in range(first, end):
            if i:
                far[i].wait_recv()
        piece = tbl.at[pl.ds(y * 16 + first, end - first)]
        for k in (2, 1, 3):
            i = g * 3 + k - 1
            sent.append(remote(piece, piece, own_s.at[i], own_r.at[i], at(0, y ^ k)))
    trial2[z] = summed(trial1, trial_copies)
    for c in sent:
        c.wait_recv()
    trial_copies = to_planes(trial2, t2_s, t2_r)

    lane_group = lax.broadcasted_iota(jnp.int32, (16, 128), 1) // 16

    def select(j, carry):
        for hp in range(2):
            acc = jnp.zeros((16, 128), F32)
            for g in range(8):
                i = j * 16 + hp * 8 + g
                moved = pltpu.roll(tbl[place[i] // 2, place[i] % 2].astype(F32), place[128 + i], 1)
                acc = jnp.where(lane_group == g, moved, acc)
            yall[j, rad, :, hp * 128:(hp + 1) * 128] = acc.astype(BF16)
        return carry

    other = (chan, rad ^ 1)
    along_x, across = {}, {}
    n_chunks = NJ // CHUNK
    for c in range(n_chunks):
        lax.fori_loop(c * CHUNK, (c + 1) * CHUNK, select, 0)
        piece = yall.at[pl.ds(c * CHUNK, CHUNK), pl.ds(rad, 1)]
        for i in (2, 1, 3):
            k = c * 3 + i - 1
            along_x[c, i] = remote(piece, piece, x_s.at[k], x_r.at[k], (chan, rad ^ (2 * i)))
        across[c, 0] = remote(piece, piece, c_s.at[c * 4], c_r.at[c * 4], other)

    out_group = lax.broadcasted_iota(jnp.int32, (16, 256), 1) // 16
    applied_r = jnp.zeros((16, 256), F32)
    for c in range(n_chunks + 1):
        if c < n_chunks:
            for i in (1, 3, 2):
                along_x[c, i].wait_recv()
                piece = yall.at[pl.ds(c * CHUNK, CHUNK), pl.ds(rad ^ (2 * i), 1)]
                across[c, i] = remote(piece, piece, c_s.at[c * 4 + i], c_r.at[c * 4 + i], other)
        if c:
            for i in range(4):
                across[c - 1, i].wait_recv()
            js = range((c - 1) * CHUNK, c * CHUNK)
            left = jnp.concatenate([hbuf[:, j].reshape(256, 128) for j in js], axis=1)
            right = yall[(c - 1) * CHUNK:c * CHUNK].reshape(CHUNK * 128, 256)
            out = jnp.dot(left, right, preferred_element_type=F32)
            for p in range(16):
                applied_r += jnp.where(out_group == p, out[p * 16:(p + 1) * 16, :], 0.0)

    turned_a = applied_r.T
    a2 = jnp.concatenate([turned_a[p * 16:(p + 1) * 16, :] for p in range(16)], axis=1)
    ad = a2 / d2

    prods = widen(lax.dot_general(jnp.concatenate([both, ad], axis=0), jnp.concatenate([a2, ad], axis=0), nt,
                                  precision=HI, preferred_element_type=F32))
    prods = jnp.where(lane < 32, prods[:16],
                      jnp.where(lane < 48, pltpu.roll(prods[16:32], 16, 1), pltpu.roll(prods[32:], 32, 1)))
    red1[y * 8 + rad] = pack(prods)
    copies = to_plane(red1, r1_s, r1_r)

    rows = lax.broadcasted_iota(jnp.int32, (16, 128), 0)

    def block(m, b):
        return (pltpu.roll(m, 128 - 16 * b, 1) if b else m)[:, :16]

    trial = unpack(summed(trial2, trial_copies))
    m = jnp.where(lane < 32, trial, jnp.where(lane == rows + 32, 1.0, 0.0))
    for i in range(16):
        pivot_row = m[i:i + 1, :] / m[i:i + 1, i:i + 1]
        m = jnp.where(rows == i, pivot_row, m - m[:, i:i + 1] * pivot_row)
    inv_b, inv_b_ttd = block(m, 2), block(m, 1)
    ttd, tdtd = block(trial, 1), block(trial, 2)

    red2[z] = summed(red1, copies)
    total = unpack(summed(red2, to_planes(red2, r2_s, r2_r)))
    dot = functools.partial(jnp.dot, precision=HI, preferred_element_type=F32)
    solved = dot(inv_b, total)
    coef = block(solved, 0)
    tda = block(total, 2)
    level = dot(jnp.concatenate([ttd, inv_b_ttd, tdtd], axis=0), coef)
    corr = block(total, 1) - level[:16]
    mixing = block(solved, 1) - level[16:32]
    inner = level[32:48] - tda
    tn = (((0,), (0,)), ((), ()))
    gram = block(total, 3) + lax.dot_general(jnp.concatenate([-tda, coef, -corr], axis=0),
                                             jnp.concatenate([coef, inner, mixing], axis=0), tn,
                                             precision=HI, preferred_element_type=F32)
    gram = gram / TOTAL_ROWS
    projected = ad - lax.dot_general(jnp.concatenate([mixing, coef], axis=0), both, tn,
                                     precision=HI, preferred_element_type=F32)
    small = (16, 16)
    diagonal = lax.broadcasted_iota(jnp.int32, small, 0) == lax.broadcasted_iota(jnp.int32, small, 1)
    ritz_ref[...] = jnp.sum(jnp.where(diagonal, coef, 0.0), axis=0, keepdims=True)

    e = jnp.concatenate([gram, jnp.where(diagonal, 1.0, 0.0), jnp.zeros((16, 96), F32)], axis=1)
    for i in range(15):
        e = e - jnp.where(rows > i, e[:, i:i + 1] / e[i:i + 1, i:i + 1], 0.0) * e[i:i + 1, :]
    pivots = jnp.sum(jnp.where(rows == lane, e, 0.0), axis=1, keepdims=True)
    inv_factor = block(e * lax.rsqrt(pivots), 1)
    new = jnp.dot(inv_factor, projected, precision=HI, preferred_element_type=F32)
    for p in range(16):
        half = new[:, (p // 8) * 128:(p // 8 + 1) * 128]
        g = p % 8
        new_ref[p] = (pltpu.roll(half, 128 - 16 * g, 1) if g else half)[:, :16]

    for c in [*far.values(), *sent, *along_x.values(), *across.values(), *sums]:
        c.wait_send()


def body(trial_block, ham_blocks, partners, stored_at, precond_diag):
    vmem = pl.BlockSpec(memory_space=pltpu.VMEM)
    hbm = pl.BlockSpec(memory_space=pltpu.HBM)
    dma = pltpu.SemaphoreType.DMA
    n_chunks = NJ // CHUNK
    counts = (5, 16, 16, 3 * len(GROUPS), 3 * len(GROUPS), 3 * n_chunks, 3 * n_chunks, 4 * n_chunks, 4 * n_chunks, *(31, 31, 16, 16) * 2)
    new_block, ritz = pl.pallas_call(
        kernel,
        out_shape=(jax.ShapeDtypeStruct((16, 16, 16), F32), jax.ShapeDtypeStruct((1, 16), F32)),
        in_specs=[hbm] * 5,
        out_specs=(vmem, vmem),
        scratch_shapes=[
            pltpu.VMEM((16, 16, 16), F32),
            pltpu.VMEM((16, 16), F32),
            pltpu.VMEM((16, 8, 16, 128), BF16),
            pltpu.SMEM((8, 16), jnp.int32),
            pltpu.SMEM((1024,), jnp.int32),
            pltpu.SMEM((256,), jnp.int32),
            pltpu.VMEM((64, 2, 16, 128), BF16),
            pltpu.VMEM((8, 8, 16, 256), BF16),
            *[pltpu.VMEM((n, 8, 128), F32) for n in (32, 16, 32, 16)],
            *[dma((n,)) for n in counts],
        ],
        compiler_params=pltpu.CompilerParams(collective_id=0, has_side_effects=True, vmem_limit_bytes=60 * 2**20),
    )(trial_block, ham_blocks, partners.T, stored_at, precond_diag)
    return new_block, ritz.reshape(16)


def solution(mesh):
    return jax.shard_map(
        body,
        mesh=mesh,
        in_specs=(
            P("chan", None, "rad"),
            P("chan", None, "rad", None),
            P("chan", None),
            P(),
            P("chan", "rad"),
        ),
        out_specs=(P("chan", None, "rad"), P()),
        check_vma=False,
    )
```

time: 62 us -> 57.2 us (0.923)
  Pallas kernels: 59.2 us -> 54.3 us
    pallas_call x1, Pallas kernels: 59.2 us -> 54.3 us  [body(): pl.pallas_call(kernel, out_shape=(jax.ShapeDtypeStruct((16, 16, 16), F32)...]
where the time goes in v3:
time: 57.2 us; the launch traced here: 57 us
  Pallas kernels  54.3 us (95%)
  local copies, waits for them, and re-layouts  2.08 us (4%)
  between operations  0.65 us (1%)
    pallas_call x1, Pallas kernels, body(): pl.pallas_call(kernel, out_shape=(jax.ShapeDtypeStruct((16, 16, 16), F32)...  54.3 us
    unnamed x4, local copies, waits for them, and re-layouts  2.08 us

profile of v3, /device:TPU:1, one launch (start us, length us, event | category | flops | bytes accessed | tf_op | source)
XLA Modules:
  0.0 57.0 jit_solution(4551283392228561041)
XLA Ops:
  0.6 54.3 %shard_map.68 = (f32[16,16,16]{2,1,0:T(8,128)}, f32[1,16]{1,0:T(1,128)}) custom-call(f32[16,16,16]{2,1,0:T(8,128)} %t_hbm.1, bf16[16,8,16,128]{3,2,1,0:T(8,128)(2,1)} %ham_hbm.1, s32[8,16]{1,0:T(8,128)} %bitcast.2, s32[1024]{0:T(1024)} %stored_hbm.1, f32[16,16]{1,0:T(8,128)} %d_hbm.1), custom_call_target="tpu_custom_call" | custom-call | tf_op jit(solution)/shard_map/pallas_call | solution.py:247
  55.0 0.0 copy-start
  55.0 1.6 %copy.9 = f32[16,16,16]{2,1,0:T(8,128)} copy(f32[16,16,16]{2,1,0:T(8,128)} %get-tuple-element.8) | data formatting | bytes 32768
  56.5 0.0 copy-done
  56.5 0.5 copy.10
Async XLA Ops:
  55.0 1.6 %copy-start = (f32[1,16]{1,0:T(1,128)S(1)}, f32[1,16]{1,0:T(1,128)}, u32[]{:S(2)}) copy-start(f32[1,16]{1,0:T(1,128)} %get-tuple-element.5) | copy-start | bytes 196

commit v4 on v3

--- a/solution.py
+++ b/solution.py
@@ -14,6 +14,7 @@
 TOTAL_ROWS = 1024.0 * 128.0
 NJ = 8
 ALONG_Z = (8, 7, 9, 6, 10, 5, 11, 4, 12, 3, 13, 2, 14, 1, 15)
+MIXED_Z = (1, 15, 2, 8, 7, 9, 14, 3, 13, 4, 6, 10, 5, 11, 12)
 IN_PLANE = sorted(((dy, dr) for dy in range(4) for dr in range(8) if dy or dr),
                   key=lambda d: -((0, 1, 2, 1)[d[0]] + (0, 1, 2, 1)[d[1] // 2]))
 GROUPS = ((0, 4), (4, 8), (8, 12), (12, 16))
@@ -25,9 +26,9 @@
 
 
 def kernel(t_hbm, ham_hbm, partners_hbm, stored_hbm, d_hbm, new_ref, ritz_ref,
-           t_ref, d_ref, hbuf, partners_ref, stored_ref, place, tbl, yall, trial1, trial2, red1, red2,
+           t_ref, d_ref, hbuf, partners_ref, stored_ref, place, tbl, yall, trial1, trial2, trial3, red1, red2,
            in_sem, far_s, far_r, own_s, own_r, x_s, x_r, c_s, c_r,
-           t1_s, t1_r, t2_s, t2_r, r1_s, r1_r, r2_s, r2_r):
+           t1_s, t1_r, t2_s, t2_r, t3_s, t3_r, r1_s, r1_r, r2_s, r2_r):
     chan = lax.axis_index("chan")
     rad = lax.axis_index("rad")
     z, y = chan // 4, chan % 4
@@ -40,8 +41,10 @@
     barrier = pltpu.get_barrier_semaphore()
     for m in ALONG_Z:
         pl.semaphore_signal(barrier, inc=1, device_id=at(m, y), device_id_type=MESH)
-    for dy, dr in IN_PLANE:
-        pl.semaphore_signal(barrier, inc=1, device_id=(z * 4 + (y ^ dy), rad ^ dr), device_id_type=MESH)
+    for k in (2, 1, 3):
+        pl.semaphore_signal(barrier, inc=1, device_id=at(0, y ^ k), device_id_type=MESH)
+    for i in range(1, 8):
+        pl.semaphore_signal(barrier, inc=1, device_id=(chan, rad ^ i), device_id_type=MESH)
     rest = [pltpu.make_async_copy(src, dst, in_sem.at[i + 1]) for i, (src, dst) in enumerate(
         ((d_hbm, d_ref), (partners_hbm, partners_ref), (stored_hbm, stored_ref), (ham_hbm, hbuf)))]
     for c in rest:
@@ -54,7 +57,7 @@
     tbl[y * 16, 0] = turned[:, :128]
     tbl[y * 16, 1] = turned[:, 128:]
 
-    pl.semaphore_wait(barrier, len(ALONG_Z) + len(IN_PLANE))
+    pl.semaphore_wait(barrier, len(ALONG_Z) + 3 + 7)
 
     def remote(src, dst, s, r, dev):
         copy = pltpu.make_async_remote_copy(src_ref=src, dst_ref=dst, send_sem=s, recv_sem=r,
@@ -63,7 +66,7 @@
         return copy
 
     far = {}
-    for m in ALONG_Z:
+    for m in MIXED_Z:
         far[by_distance(16 - m)] = remote(tbl.at[pl.ds(y * 16, 1)], tbl.at[pl.ds(y * 16 + by_distance(16 - m), 1)],
                                           far_s.at[m], far_r.at[m], at(m, y))
 
@@ -89,6 +92,14 @@
         piece = buf.at[pl.ds(y * 8 + rad, 1)]
         return [remote(piece, piece, s.at[i], r.at[i], (z * 4 + (y ^ dy), rad ^ dr))
                 for i, (dy, dr) in enumerate(IN_PLANE)]
+
+    def to_rad(buf, s, r):
+        piece = buf.at[pl.ds(rad, 1)]
+        return [remote(piece, piece, s.at[i - 1], r.at[i - 1], (chan, rad ^ i)) for i in range(1, 8)]
+
+    def to_y(buf, s, r):
+        piece = buf.at[pl.ds(y, 1)]
+        return [remote(piece, piece, s.at[k - 1], r.at[k - 1], at(0, y ^ k)) for k in (2, 1, 3)]
 
     def to_planes(buf, s, r):
         piece = buf.at[pl.ds(z, 1)]
@@ -109,8 +120,8 @@
     both = jnp.concatenate([t2, td], axis=0)
     prods = widen(lax.dot_general(both, both, nt, precision=HI, preferred_element_type=F32))
     prods = jnp.where(lane < 32, prods[:16], jnp.where(lane < 48, pltpu.roll(prods[16:], 16, 1), 0.0))
-    trial1[y * 8 + rad] = pack(prods)
-    trial_copies = to_plane(trial1, t1_s, t1_r)
+    trial1[rad] = pack(prods)
+    trial_copies = to_rad(trial1, t1_s, t1_r)
 
     def locate(j, carry):
         for p in range(16):
@@ -132,10 +143,10 @@
         for k in (2, 1, 3):
             i = g * 3 + k - 1
             sent.append(remote(piece, piece, own_s.at[i], own_r.at[i], at(0, y ^ k)))
-    trial2[z] = summed(trial1, trial_copies)
+    trial2[y] = summed(trial1, trial_copies)
+    trial_copies = to_y(trial2, t2_s, t2_r)
     for c in sent:
         c.wait_recv()
-    trial_copies = to_planes(trial2, t2_s, t2_r)
 
     lane_group = lax.broadcasted_iota(jnp.int32, (16, 128), 1) // 16
 
@@ -160,6 +171,8 @@
             along_x[c, i] = remote(piece, piece, x_s.at[k], x_r.at[k], (chan, rad ^ (2 * i)))
         across[c, 0] = remote(piece, piece, c_s.at[c * 4], c_r.at[c * 4], other)
 
+    trial3[z] = summed(trial2, trial_copies)
+    trial_copies = to_planes(trial3, t3_s, t3_r)
     out_group = lax.broadcasted_iota(jnp.int32, (16, 256), 1) // 16
     applied_r = jnp.zeros((16, 256), F32)
     for c in range(n_chunks + 1):
@@ -194,7 +207,7 @@
     def block(m, b):
         return (pltpu.roll(m, 128 - 16 * b, 1) if b else m)[:, :16]
 
-    trial = unpack(summed(trial2, trial_copies))
+    trial = unpack(summed(trial3, trial_copies))
     m = jnp.where(lane < 32, trial, jnp.where(lane == rows + 32, 1.0, 0.0))
     for i in range(16):
         pivot_row = m[i:i + 1, :] / m[i:i + 1, i:i + 1]
@@ -243,7 +256,7 @@
     hbm = pl.BlockSpec(memory_space=pltpu.HBM)
     dma = pltpu.SemaphoreType.DMA
     n_chunks = NJ // CHUNK
-    counts = (5, 16, 16, 3 * len(GROUPS), 3 * len(GROUPS), 3 * n_chunks, 3 * n_chunks, 4 * n_chunks, 4 * n_chunks, *(31, 31, 16, 16) * 2)
+    counts = (5, 16, 16, 3 * len(GROUPS), 3 * len(GROUPS), 3 * n_chunks, 3 * n_chunks, 4 * n_chunks, 4 * n_chunks, 7, 7, 3, 3, 16, 16, 31, 31, 16, 16)
     new_block, ritz = pl.pallas_call(
         kernel,
         out_shape=(jax.ShapeDtypeStruct((16, 16, 16), F32), jax.ShapeDtypeStruct((1, 16), F32)),
@@ -258,7 +271,7 @@
             pltpu.SMEM((256,), jnp.int32),
             pltpu.VMEM((64, 2, 16, 128), BF16),
             pltpu.VMEM((8, 8, 16, 256), BF16),
-            *[pltpu.VMEM((n, 8, 128), F32) for n in (32, 16, 32, 16)],
+            *[pltpu.VMEM((n, 8, 128), F32) for n in (8, 4, 16, 32, 16)],
             *[dma((n,)) for n in counts],
         ],
         compiler_params=pltpu.CompilerParams(collective_id=0, has_side_effects=True, vmem_limit_bytes=60 * 2**20),

time: 57.2 us -> 56.6 us (0.990)
  Pallas kernels: 54.3 us -> 53.7 us
    pallas_call x1, Pallas kernels: 54.3 us -> 53.7 us  [body(): pl.pallas_call(kernel, out_shape=(jax.ShapeDtypeStruct((16, 16, 16), F32)...]
where the time goes in v4:
time: 56.6 us; the launch traced here: 56.4 us
  Pallas kernels  53.7 us (95%)
  local copies, waits for them, and re-layouts  2.08 us (4%)
  between operations  0.65 us (1%)
    pallas_call x1, Pallas kernels, body(): pl.pallas_call(kernel, out_shape=(jax.ShapeDtypeStruct((16, 16, 16), F32)...  53.7 us
    unnamed x4, local copies, waits for them, and re-layouts  2.08 us

profile of v4, /device:TPU:1, one launch (start us, length us, event | category | flops | bytes accessed | tf_op | source)
XLA Modules:
  0.0 56.4 jit_solution(4398834427891105780)
XLA Ops:
  0.6 53.7 %shard_map.68 = (f32[16,16,16]{2,1,0:T(8,128)}, f32[1,16]{1,0:T(1,128)}) custom-call(f32[16,16,16]{2,1,0:T(8,128)} %t_hbm.1, bf16[16,8,16,128]{3,2,1,0:T(8,128)(2,1)} %ham_hbm.1, s32[8,16]{1,0:T(8,128)} %bitcast.2, s32[1024]{0:T(1024)} %stored_hbm.1, f32[16,16]{1,0:T(8,128)} %d_hbm.1), custom_call_target="tpu_custom_call" | custom-call | tf_op jit(solution)/shard_map/pallas_call | solution.py:260
  54.3 0.0 copy-start
  54.3 1.6 %copy.9 = f32[16,16,16]{2,1,0:T(8,128)} copy(f32[16,16,16]{2,1,0:T(8,128)} %get-tuple-element.8) | data formatting | bytes 32768
  55.9 0.0 copy-done
  55.9 0.5 copy.10
Async XLA Ops:
  54.3 1.6 %copy-start = (f32[1,16]{1,0:T(1,128)S(1)}, f32[1,16]{1,0:T(1,128)}, u32[]{:S(2)}) copy-start(f32[1,16]{1,0:T(1,128)} %get-tuple-element.5) | copy-start | bytes 196

commit v5 on v4

--- a/solution.py
+++ b/solution.py
@@ -13,16 +13,11 @@
 BF16 = jnp.bfloat16
 TOTAL_ROWS = 1024.0 * 128.0
 NJ = 8
+NEAR_Z = (4, 12, 3, 13, 2, 14, 1, 15)
 ALONG_Z = (8, 7, 9, 6, 10, 5, 11, 4, 12, 3, 13, 2, 14, 1, 15)
-MIXED_Z = (1, 15, 2, 8, 7, 9, 14, 3, 13, 4, 6, 10, 5, 11, 12)
 IN_PLANE = sorted(((dy, dr) for dy in range(4) for dr in range(8) if dy or dr),
                   key=lambda d: -((0, 1, 2, 1)[d[0]] + (0, 1, 2, 1)[d[1] // 2]))
-GROUPS = ((0, 4), (4, 8), (8, 12), (12, 16))
 CHUNK = 4
-
-
-def by_distance(d):
-    return 2 * d - 1 if 0 < d <= 8 else 2 * (16 - d) % 32
 
 
 def kernel(t_hbm, ham_hbm, partners_hbm, stored_hbm, d_hbm, new_ref, ritz_ref,
@@ -39,7 +34,7 @@
     t_copy = pltpu.make_async_copy(t_hbm, t_ref, in_sem.at[0])
     t_copy.start()
     barrier = pltpu.get_barrier_semaphore()
-    for m in ALONG_Z:
+    for m in NEAR_Z:
         pl.semaphore_signal(barrier, inc=1, device_id=at(m, y), device_id_type=MESH)
     for k in (2, 1, 3):
         pl.semaphore_signal(barrier, inc=1, device_id=at(0, y ^ k), device_id_type=MESH)
@@ -57,7 +52,7 @@
     tbl[y * 16, 0] = turned[:, :128]
     tbl[y * 16, 1] = turned[:, 128:]
 
-    pl.semaphore_wait(barrier, len(ALONG_Z) + 3 + 7)
+    pl.semaphore_wait(barrier, len(NEAR_Z) + 3 + 7)
 
     def remote(src, dst, s, r, dev):
         copy = pltpu.make_async_remote_copy(src_ref=src, dst_ref=dst, send_sem=s, recv_sem=r,
@@ -65,10 +60,12 @@
         copy.start()
         return copy
 
+    def blocks(first, end):
+        return tbl.at[pl.ds(y * 16 + first, end - first)]
+
     far = {}
-    for m in MIXED_Z:
-        far[by_distance(16 - m)] = remote(tbl.at[pl.ds(y * 16, 1)], tbl.at[pl.ds(y * 16 + by_distance(16 - m), 1)],
-                                          far_s.at[m], far_r.at[m], at(m, y))
+    for m in NEAR_Z:
+        far[16 - m] = remote(blocks(0, 1), blocks(16 - m, 17 - m), far_s.at[m], far_r.at[m], at(m, y))
 
     for c in rest:
         c.wait()
@@ -127,24 +124,34 @@
         for p in range(16):
             row = stored_ref[partners_ref[j, p]]
             ahead = (row // 64 - z + 16) % 16
-            order = jnp.where(ahead > 8, 32 - 2 * ahead, jnp.maximum(2 * ahead - 1, 0))
-            place[j * 16 + p] = ((row // 16) % 4 * 16 + order) * 2 + (row // 8) % 2
+            place[j * 16 + p] = ((row // 16) % 4 * 16 + ahead) * 2 + (row // 8) % 2
             place[128 + j * 16 + p] = ((p - row + 16) % 8) * 16
         return carry
 
     lax.fori_loop(0, NJ, locate, 0)
 
-    sent = []
-    for g, (first, end) in enumerate(GROUPS):
-        for i in range(first, end):
-            if i:
-                far[i].wait_recv()
-        piece = tbl.at[pl.ds(y * 16 + first, end - first)]
+    sent, passed = [], []
+
+    def along_y(first, end, g):
         for k in (2, 1, 3):
             i = g * 3 + k - 1
-            sent.append(remote(piece, piece, own_s.at[i], own_r.at[i], at(0, y ^ k)))
+            sent.append(remote(blocks(first, end), blocks(first, end), own_s.at[i], own_r.at[i], at(0, y ^ k)))
+
+    for i in (13, 14, 15):
+        far[i].wait_recv()
+    passed.append(remote(blocks(13, 16), blocks(9, 12), far_s.at[5], far_r.at[5], at(4, y)))
+    for i in (1, 2, 3, 4):
+        far[i].wait_recv()
+    passed.append(remote(blocks(1, 5), blocks(5, 9), far_s.at[6], far_r.at[6], at(-4, y)))
+    along_y(0, 5, 0)
+    far[12].wait_recv()
+    along_y(12, 16, 1)
     trial2[y] = summed(trial1, trial_copies)
     trial_copies = to_y(trial2, t2_s, t2_r)
+    passed[0].wait_recv()
+    along_y(9, 12, 2)
+    passed[1].wait_recv()
+    along_y(5, 9, 3)
     for c in sent:
         c.wait_recv()
 
@@ -247,7 +254,7 @@
         g = p % 8
         new_ref[p] = (pltpu.roll(half, 128 - 16 * g, 1) if g else half)[:, :16]
 
-    for c in [*far.values(), *sent, *along_x.values(), *across.values(), *sums]:
+    for c in [*far.values(), *passed, *sent, *along_x.values(), *across.values(), *sums]:
         c.wait_send()
 
 
@@ -256,7 +263,7 @@
     hbm = pl.BlockSpec(memory_space=pltpu.HBM)
     dma = pltpu.SemaphoreType.DMA
     n_chunks = NJ // CHUNK
-    counts = (5, 16, 16, 3 * len(GROUPS), 3 * len(GROUPS), 3 * n_chunks, 3 * n_chunks, 4 * n_chunks, 4 * n_chunks, 7, 7, 3, 3, 16, 16, 31, 31, 16, 16)
+    counts = (5, 16, 16, 12, 12, 3 * n_chunks, 3 * n_chunks, 4 * n_chunks, 4 * n_chunks, 7, 7, 3, 3, 16, 16, 31, 31, 16, 16)
     new_block, ritz = pl.pallas_call(
         kernel,
         out_shape=(jax.ShapeDtypeStruct((16, 16, 16), F32), jax.ShapeDtypeStruct((1, 16), F32)),

time: 56.6 us -> 54.2 us (0.958)
  Pallas kernels: 53.7 us -> 51.4 us
    pallas_call x1, Pallas kernels: 53.7 us -> 51.4 us  [body(): pl.pallas_call(kernel, out_shape=(jax.ShapeDtypeStruct((16, 16, 16), F32)...]
where the time goes in v5:
time: 54.2 us; the launch traced here: 54.1 us
  Pallas kernels  51.4 us (95%)
  local copies, waits for them, and re-layouts  2.08 us (4%)
  between operations  0.65 us (1%)
    pallas_call x1, Pallas kernels, body(): pl.pallas_call(kernel, out_shape=(jax.ShapeDtypeStruct((16, 16, 16), F32)...  51.4 us
    unnamed x4, local copies, waits for them, and re-layouts  2.08 us

profile of v5, /device:TPU:1, one launch (start us, length us, event | category | flops | bytes accessed | tf_op | source)
XLA Modules:
  0.0 54.1 jit_solution(15531589778117092966)
XLA Ops:
  0.6 51.4 %shard_map.68 = (f32[16,16,16]{2,1,0:T(8,128)}, f32[1,16]{1,0:T(1,128)}) custom-call(f32[16,16,16]{2,1,0:T(8,128)} %t_hbm.1, bf16[16,8,16,128]{3,2,1,0:T(8,128)(2,1)} %ham_hbm.1, s32[8,16]{1,0:T(8,128)} %bitcast.2, s32[1024]{0:T(1024)} %stored_hbm.1, f32[16,16]{1,0:T(8,128)} %d_hbm.1), custom_call_target="tpu_custom_call" | custom-call | tf_op jit(solution)/shard_map/pallas_call | solution.py:267
  52.0 0.0 copy-start
  52.0 1.6 %copy.9 = f32[16,16,16]{2,1,0:T(8,128)} copy(f32[16,16,16]{2,1,0:T(8,128)} %get-tuple-element.8) | data formatting | bytes 32768
  53.6 0.0 copy-done
  53.6 0.5 copy.10
Async XLA Ops:
  52.0 1.6 %copy-start = (f32[1,16]{1,0:T(1,128)S(1)}, f32[1,16]{1,0:T(1,128)}, u32[]{:S(2)}) copy-start(f32[1,16]{1,0:T(1,128)} %get-tuple-element.5) | copy-start | bytes 196

commit v6 on v5

--- a/solution.py
+++ b/solution.py
@@ -20,7 +20,7 @@
 CHUNK = 4
 
 
-def kernel(t_hbm, ham_hbm, partners_hbm, stored_hbm, d_hbm, new_ref, ritz_ref,
+def kernel(t_hbm, ham_hbm, partners_hbm, stored_hbm, d_hbm, total_ref, inverse_ref, trial_ref, states_ref,
            t_ref, d_ref, hbuf, partners_ref, stored_ref, place, tbl, yall, trial1, trial2, trial3, red1, red2,
            in_sem, far_s, far_r, own_s, own_r, x_s, x_r, c_s, c_r,
            t1_s, t1_r, t2_s, t2_r, t3_s, t3_r, r1_s, r1_r, r2_s, r2_r):
@@ -137,21 +137,19 @@
             i = g * 3 + k - 1
             sent.append(remote(blocks(first, end), blocks(first, end), own_s.at[i], own_r.at[i], at(0, y ^ k)))
 
-    for i in (13, 14, 15):
-        far[i].wait_recv()
-    passed.append(remote(blocks(13, 16), blocks(9, 12), far_s.at[5], far_r.at[5], at(4, y)))
-    for i in (1, 2, 3, 4):
-        far[i].wait_recv()
-    passed.append(remote(blocks(1, 5), blocks(5, 9), far_s.at[6], far_r.at[6], at(-4, y)))
+    for n, (take, first, end, to, dz) in enumerate((
+            ((15, 14), 14, 16, 10, 4), ((1, 2), 1, 3, 5, -4), ((13,), 13, 14, 9, 4), ((3, 4), 3, 5, 7, -4))):
+        for i in take:
+            far[i].wait_recv()
+        passed.append(remote(blocks(first, end), blocks(to, to + end - first), far_s.at[5 + n], far_r.at[5 + n], at(dz, y)))
     along_y(0, 5, 0)
     far[12].wait_recv()
     along_y(12, 16, 1)
     trial2[y] = summed(trial1, trial_copies)
     trial_copies = to_y(trial2, t2_s, t2_r)
-    passed[0].wait_recv()
-    along_y(9, 12, 2)
-    passed[1].wait_recv()
-    along_y(5, 9, 3)
+    for n, (first, end) in enumerate(((10, 12), (5, 7), (9, 10), (7, 9))):
+        passed[n].wait_recv()
+        along_y(first, end, 2 + n)
     for c in sent:
         c.wait_recv()
 
@@ -224,6 +222,26 @@
 
     red2[z] = summed(red1, copies)
     total = unpack(summed(red2, to_planes(red2, r2_s, r2_r)))
+    total_ref[...] = total
+    inverse_ref[...] = m
+    trial_ref[...] = trial
+    states_ref[...] = jnp.concatenate([both, ad], axis=0)
+
+    for c in [*far.values(), *passed, *sent, *along_x.values(), *across.values(), *sums]:
+        c.wait_send()
+
+
+def finish(total_ref, inverse_ref, trial_ref, states_ref, new_ref, ritz_ref):
+    lane = lax.broadcasted_iota(jnp.int32, (16, 128), 1)
+    rows = lax.broadcasted_iota(jnp.int32, (16, 128), 0)
+
+    def block(m, b):
+        return (pltpu.roll(m, 128 - 16 * b, 1) if b else m)[:, :16]
+
+    total = total_ref[...]
+    inv_b, inv_b_ttd = block(inverse_ref[...], 2), block(inverse_ref[...], 1)
+    ttd, tdtd = block(trial_ref[...], 1), block(trial_ref[...], 2)
+    both, ad = states_ref[:32], states_ref[32:]
     dot = functools.partial(jnp.dot, precision=HI, preferred_element_type=F32)
     solved = dot(inv_b, total)
     coef = block(solved, 0)
@@ -241,7 +259,7 @@
                                      precision=HI, preferred_element_type=F32)
     small = (16, 16)
     diagonal = lax.broadcasted_iota(jnp.int32, small, 0) == lax.broadcasted_iota(jnp.int32, small, 1)
-    ritz_ref[...] = jnp.sum(jnp.where(diagonal, coef, 0.0), axis=0, keepdims=True)
+    ritz_ref[...] = jnp.sum(jnp.where(diagonal, coef, 0.0), axis=0)
 
     e = jnp.concatenate([gram, jnp.where(diagonal, 1.0, 0.0), jnp.zeros((16, 96), F32)], axis=1)
     for i in range(15):
@@ -254,21 +272,19 @@
         g = p % 8
         new_ref[p] = (pltpu.roll(half, 128 - 16 * g, 1) if g else half)[:, :16]
 
-    for c in [*far.values(), *passed, *sent, *along_x.values(), *across.values(), *sums]:
-        c.wait_send()
-
 
 def body(trial_block, ham_blocks, partners, stored_at, precond_diag):
     vmem = pl.BlockSpec(memory_space=pltpu.VMEM)
     hbm = pl.BlockSpec(memory_space=pltpu.HBM)
     dma = pltpu.SemaphoreType.DMA
     n_chunks = NJ // CHUNK
-    counts = (5, 16, 16, 12, 12, 3 * n_chunks, 3 * n_chunks, 4 * n_chunks, 4 * n_chunks, 7, 7, 3, 3, 16, 16, 31, 31, 16, 16)
-    new_block, ritz = pl.pallas_call(
+    counts = (5, 16, 16, 18, 18, 3 * n_chunks, 3 * n_chunks, 4 * n_chunks, 4 * n_chunks, 7, 7, 3, 3, 16, 16, 31, 31, 16, 16)
+    vm4 = [vmem] * 4
+    parts = pl.pallas_call(
         kernel,
-        out_shape=(jax.ShapeDtypeStruct((16, 16, 16), F32), jax.ShapeDtypeStruct((1, 16), F32)),
+        out_shape=[jax.ShapeDtypeStruct(shape, F32) for shape in ((16, 128), (16, 128), (16, 128), (48, 256))],
         in_specs=[hbm] * 5,
-        out_specs=(vmem, vmem),
+        out_specs=vm4,
         scratch_shapes=[
             pltpu.VMEM((16, 16, 16), F32),
             pltpu.VMEM((16, 16), F32),
@@ -283,7 +299,14 @@
         ],
         compiler_params=pltpu.CompilerParams(collective_id=0, has_side_effects=True, vmem_limit_bytes=60 * 2**20),
     )(trial_block, ham_blocks, partners.T, stored_at, precond_diag)
-    return new_block, ritz.reshape(16)
+    new_block, ritz = pl.pallas_call(
+        finish,
+        out_shape=(jax.ShapeDtypeStruct((16, 16, 16), F32), jax.ShapeDtypeStruct((16,), F32)),
+        in_specs=vm4,
+        out_specs=(vmem, vmem),
+        compiler_params=pltpu.CompilerParams(vmem_limit_bytes=60 * 2**20),
+    )(*parts)
+    return new_block, ritz
 
 
 def solution(mesh):

time: 54.2 us -> 53.1 us (0.980)
  local copies, waits for them, and re-layouts: 2.08 us -> 0 us
  Pallas kernels: 51.4 us -> 52.3 us
    unnamed x4 -> x0, local copies, waits for them, and re-layouts: 2.08 us -> none
    pallas_call x1 -> x2, Pallas kernels: 51.4 us -> 52.3 us  [the longest x1 48.6 us: body(): pl.pallas_call(kernel, out_shape=[jax.ShapeDtypeStruct(shape, F32) for sh...]
where the time goes in v6:
time: 53.1 us; the launch traced here: 52.9 us
  Pallas kernels  52.3 us (98%)
  between operations  0.64 us (1%)
    pallas_call x1, Pallas kernels, body(): pl.pallas_call(kernel, out_shape=[jax.ShapeDtypeStruct(shape, F32) for sh...  48.6 us
    pallas_call x1, Pallas kernels, body(): pl.pallas_call(finish, out_shape=(jax.ShapeDtypeStruct((16, 16, 16), F32)...  3.71 us

profile of v6, /device:TPU:1, one launch (start us, length us, event | category | flops | bytes accessed | tf_op | source)
XLA Modules:
  0.0 52.9 jit_solution(5464671834782985067)
XLA Ops:
  0.6 48.6 %shard_map.68 = (f32[16,128]{1,0:T(8,128)}, f32[16,128]{1,0:T(8,128)}, f32[16,128]{1,0:T(8,128)}, f32[48,256]{1,0:T(8,128)}) custom-call(f32[16,16,16]{2,1,0:T(8,128)} %t_hbm.1, bf16[16,8,16,128]{3,2,1,0:T(8,128)(2,1)} %ham_hbm.1, s32[8,16]{1,0:T(8,128)} %bitcast.1, s32[1024]{0:T(1024)} %stored_hbm.1, f32[16,16]{1,0:T(8,128)} %d_hbm.1), custom_call_target="tpu_custom_call" | custom-call | tf_op jit(solution)/shard_map/pallas_call | solution.py:283
  49.2 3.7 %shard_map.69 = (f32[16,16,16]{2,1,0:T(8,128)}, f32[16]{0:T(128)}) custom-call(f32[16,128]{1,0:T(8,128)} %get-tuple-element.6.total_ref, f32[16,128]{1,0:T(8,128)} %get-tuple-element.7.inverse_ref, f32[16,128]{1,0:T(8,128)} %get-tuple-element.8.trial_ref, f32[48,256]{1,0:T(8,128)} %get-tuple-element.9.states_ref), custom_call_target="tpu_custom_call" | custom-call | tf_op jit(solution)/shard_map/pallas_call | solution.py:302

commit v7 on v6

--- a/solution.py
+++ b/solution.py
@@ -221,13 +221,16 @@
     ttd, tdtd = block(trial, 1), block(trial, 2)
 
     red2[z] = summed(red1, copies)
-    total = unpack(summed(red2, to_planes(red2, r2_s, r2_r)))
+    copies = to_planes(red2, r2_s, r2_r)
+    for c in [*far.values(), *passed, *sent, *along_x.values(), *across.values(), *sums]:
+        c.wait_send()
+    total = unpack(summed(red2, copies))
     total_ref[...] = total
     inverse_ref[...] = m
     trial_ref[...] = trial
     states_ref[...] = jnp.concatenate([both, ad], axis=0)
 
-    for c in [*far.values(), *passed, *sent, *along_x.values(), *across.values(), *sums]:
+    for c in copies:
         c.wait_send()
 
 
@@ -263,7 +266,7 @@
 
     e = jnp.concatenate([gram, jnp.where(diagonal, 1.0, 0.0), jnp.zeros((16, 96), F32)], axis=1)
     for i in range(15):
-        e = e - jnp.where(rows > i, e[:, i:i + 1] / e[i:i + 1, i:i + 1], 0.0) * e[i:i + 1, :]
+        e = e - jnp.where(rows > i, e[:, i:i + 1], 0.0) * (e[i:i + 1, :] / e[i:i + 1, i:i + 1])
     pivots = jnp.sum(jnp.where(rows == lane, e, 0.0), axis=1, keepdims=True)
     inv_factor = block(e * lax.rsqrt(pivots), 1)
     new = jnp.dot(inv_factor, projected, precision=HI, preferred_element_type=F32)

time: 53.1 us -> 52.9 us (level)
  no operation moved by 1% of the time
where the time goes in v7:
time: 52.9 us; the launch traced here: 52.8 us
  Pallas kernels  52.1 us (98%)
  between operations  0.64 us (1%)
    pallas_call x1, Pallas kernels, body(): pl.pallas_call(kernel, out_shape=[jax.ShapeDtypeStruct(shape, F32) for sh...  48.4 us
    pallas_call x1, Pallas kernels, body(): pl.pallas_call(finish, out_shape=(jax.ShapeDtypeStruct((16, 16, 16), F32)...  3.71 us

profile of v7, /device:TPU:1, one launch (start us, length us, event | category | flops | bytes accessed | tf_op | source)
XLA Modules:
  0.0 52.8 jit_solution(15489559664766192125)
XLA Ops:
  0.6 48.4 %shard_map.68 = (f32[16,128]{1,0:T(8,128)}, f32[16,128]{1,0:T(8,128)}, f32[16,128]{1,0:T(8,128)}, f32[48,256]{1,0:T(8,128)}) custom-call(f32[16,16,16]{2,1,0:T(8,128)} %t_hbm.1, bf16[16,8,16,128]{3,2,1,0:T(8,128)(2,1)} %ham_hbm.1, s32[8,16]{1,0:T(8,128)} %bitcast.1, s32[1024]{0:T(1024)} %stored_hbm.1, f32[16,16]{1,0:T(8,128)} %d_hbm.1), custom_call_target="tpu_custom_call" | custom-call | tf_op jit(solution)/shard_map/pallas_call | solution.py:286
  49.0 3.7 %shard_map.69 = (f32[16,16,16]{2,1,0:T(8,128)}, f32[16]{0:T(128)}) custom-call(f32[16,128]{1,0:T(8,128)} %get-tuple-element.6.total_ref, f32[16,128]{1,0:T(8,128)} %get-tuple-element.7.inverse_ref, f32[16,128]{1,0:T(8,128)} %get-tuple-element.8.trial_ref, f32[48,256]{1,0:T(8,128)} %get-tuple-element.9.states_ref), custom_call_target="tpu_custom_call" | custom-call | tf_op jit(solution)/shard_map/pallas_call | solution.py:305

commit v8 on v7

--- a/solution.py
+++ b/solution.py
@@ -145,11 +145,11 @@
     along_y(0, 5, 0)
     far[12].wait_recv()
     along_y(12, 16, 1)
-    trial2[y] = summed(trial1, trial_copies)
-    trial_copies = to_y(trial2, t2_s, t2_r)
     for n, (first, end) in enumerate(((10, 12), (5, 7), (9, 10), (7, 9))):
         passed[n].wait_recv()
         along_y(first, end, 2 + n)
+    trial2[y] = summed(trial1, trial_copies)
+    trial_copies = to_y(trial2, t2_s, t2_r)
     for c in sent:
         c.wait_recv()
 

time: 52.9 us -> 52.9 us (level)
  no operation moved by 1% of the time
where the time goes in v8:
time: 52.9 us; the launch traced here: 52.8 us
  Pallas kernels  52.1 us (98%)
  between operations  0.64 us (1%)
    pallas_call x1, Pallas kernels, body(): pl.pallas_call(kernel, out_shape=[jax.ShapeDtypeStruct(shape, F32) for sh...  48.4 us
    pallas_call x1, Pallas kernels, body(): pl.pallas_call(finish, out_shape=(jax.ShapeDtypeStruct((16, 16, 16), F32)...  3.71 us

profile of v8, /device:TPU:1, one launch (start us, length us, event | category | flops | bytes accessed | tf_op | source)
XLA Modules:
  0.0 52.8 jit_solution(15290751954197305179)
XLA Ops:
  0.6 48.4 %shard_map.68 = (f32[16,128]{1,0:T(8,128)}, f32[16,128]{1,0:T(8,128)}, f32[16,128]{1,0:T(8,128)}, f32[48,256]{1,0:T(8,128)}) custom-call(f32[16,16,16]{2,1,0:T(8,128)} %t_hbm.1, bf16[16,8,16,128]{3,2,1,0:T(8,128)(2,1)} %ham_hbm.1, s32[8,16]{1,0:T(8,128)} %bitcast.1, s32[1024]{0:T(1024)} %stored_hbm.1, f32[16,16]{1,0:T(8,128)} %d_hbm.1), custom_call_target="tpu_custom_call" | custom-call | tf_op jit(solution)/shard_map/pallas_call | solution.py:286
  49.0 3.7 %shard_map.69 = (f32[16,16,16]{2,1,0:T(8,128)}, f32[16]{0:T(128)}) custom-call(f32[16,128]{1,0:T(8,128)} %get-tuple-element.6.total_ref, f32[16,128]{1,0:T(8,128)} %get-tuple-element.7.inverse_ref, f32[16,128]{1,0:T(8,128)} %get-tuple-element.8.trial_ref, f32[48,256]{1,0:T(8,128)} %get-tuple-element.9.states_ref), custom_call_target="tpu_custom_call" | custom-call | tf_op jit(solution)/shard_map/pallas_call | solution.py:305
